TPU v7x, 512 devices: a whole 4x8x8 slice. The times are simulated.
512 devices in a mesh: section: 16 (over x_hi, y), expert: 8 (over z), dp: 4 (over x_lo, core).
Axes of the slice: x: 4 (x_hi: 2, x_lo: 2; x = x_hi * 2 + x_lo), y: 8, z: 8, core: 2. Of those that a mesh axis runs over, the one named last changes fastest.
Arguments:
- tokens: bfloat16 [2048, 6144], P('section', ('dp', 'expert')), may hold values from -6 to 6
- norm_gain: float32 [6144], P(('dp', 'expert')), may hold values from 0.25 to 1.75
- routes: int32 [2048, 2], P('section'), may hold values from 0 to 7, all different within a row; in each aligned block of 128 rows (0 to 127, 128 to 255, ...) at most 48 rows name the same one
- gates: float32 [2048, 2], P('section'), may hold values from 0.1 to 1
- w_gate: bfloat16 [8, 6144, 8192], P('expert', 'dp', 'section'), may hold values from -0.078125 to 0.078125
- w_up: bfloat16 [8, 6144, 8192], P('expert', 'dp', 'section'), may hold values from -0.078125 to 0.078125
- w_down: bfloat16 [8, 8192, 6144], P('expert', 'section', 'dp'), may hold values from -0.0625 to 0.0625
Outputs:
- mixed: bfloat16 [2048, 6144], P('section', ('dp', 'expert'))
Inputs may be any that keep to these rules, and one draw needn't show every extreme that they name: `routes`: each token names two different experts. Within each aligned block of 128 rows no expert is named by more than 48 rows, and in some block one expert is named by exactly 48.
All inputs are finite; a program needn't handle non-finite values.
Results may differ from a plain program's by a relative error of at most 0.015.
Values may be sent and summed in bfloat16 or wider, within the bound.
A program may use at most 64 MiB of HBM per device.

v0:
```python
import jax
import jax.numpy as jnp
from jax import lax
from jax.sharding import PartitionSpec as P

D = 6144


def local(tokens, norm_gain, routes, gates, w_gate, w_up, w_down):
    row_count, piece_width = tokens.shape
    expert_count = lax.axis_size("expert")
    capacity = min(row_count, max(2, 3 * row_count // expert_count))
    stream = tokens.astype(jnp.float32)
    squares = lax.psum(jnp.sum(stream * stream, axis=-1), ("expert", "dp"))
    scale = lax.rsqrt(squares / D + 1e-05)[:, None]
    normed = (stream * scale * norm_gain[None, :]).astype(jnp.bfloat16)
    flat_routes = routes.reshape(-1)
    onehot = (flat_routes[:, None] == jnp.arange(expert_count, dtype=jnp.int32)[None, :]).astype(
        jnp.int32
    )
    before = jnp.cumsum(onehot, axis=0) - onehot
    slot_number = jnp.sum(before * onehot, axis=1)
    position = flat_routes * capacity + slot_number
    owner = jnp.arange(2 * row_count, dtype=jnp.int32) // 2
    table = jnp.full((expert_count * capacity,), row_count, jnp.int32).at[position].set(owner)
    padded = jnp.concatenate([normed, jnp.zeros((1, piece_width), jnp.bfloat16)], 0)
    picked = padded[table].reshape(expert_count, capacity, piece_width)
    gate_here = w_gate[0]
    up_here = w_up[0]
    down_here = w_down[0]
    arrived = lax.all_to_all(picked, "expert", split_axis=0, concat_axis=0, tiled=True)
    senders, slot_count, part_width = arrived.shape
    joined = arrived.transpose(1, 0, 2).reshape(slot_count, senders * part_width)
    piece = lax.all_gather(joined, "section", axis=0, tiled=True)
    gate_part = jnp.dot(piece, gate_here, preferred_element_type=jnp.float32)
    up_part = jnp.dot(piece, up_here, preferred_element_type=jnp.float32)
    paired = jnp.stack([gate_part, up_part], 1)
    summed = lax.psum(paired.astype(jnp.bfloat16), "dp").astype(jnp.float32)
    hidden = (jax.nn.silu(summed[:, 0]) * summed[:, 1]).astype(jnp.bfloat16)
    answer = lax.psum_scatter(
        jnp.dot(hidden, down_here, preferred_element_type=jnp.float32).astype(jnp.bfloat16),
        "section",
        scatter_dimension=0,
        tiled=True,
    )
    answer = answer.reshape(slot_count, senders, part_width).transpose(1, 0, 2)
    back = lax.all_to_all(answer, "expert", split_axis=0, concat_axis=0, tiled=True)
    slot_rows = back.reshape(expert_count * capacity, piece_width)
    rows_back = slot_rows[position].astype(jnp.float32).reshape(row_count, 2, piece_width)
    mixed = (stream + jnp.sum(gates[:, :, None] * rows_back, axis=1)).astype(jnp.bfloat16)
    return mixed


def solution(mesh):
    in_specs = (
        P("section", ("dp", "expert")),
        P(("dp", "expert")),
        P("section", None),
        P("section", None),
        P("expert", "dp", "section"),
        P("expert", "dp", "section"),
        P("expert", "section", "dp"),
    )
    out_specs = P("section", ("dp", "expert"))
    return jax.shard_map(local, mesh=mesh, in_specs=in_specs, out_specs=out_specs, check_vma=False)
```

profile of v0, /device:TPU:1, one launch (start us, length us, event | category | flops | bytes accessed | tf_op | source)
XLA Modules:
  0.0 487.3 jit_solution(15713696599738215817)
XLA Ops:
  6.5 0.0 copy-start
  6.5 0.0 all-gather.2.cloned.1.call-start
  6.5 0.9 copy.23
  7.4 0.1 eq.29
  7.6 0.1 eq.25
  7.7 0.7 broadcast_multiply_fusion
  8.4 0.6 reduce-window.6
  9.0 0.2 slice_reduce_fusion
  9.3 0.1 copy.22
  9.4 0.1 mul.63
  9.5 0.1 fusion.25
  9.6 1.4 scatter_custom_fusion
  11.0 0.9 copy.20
  12.0 0.1 fusion.20
  12.1 60.1 %psum.14 = f32[128]{0:T(128)S(1)} all-reduce(f32[128]{0:T(128)S(1)} %fusion.20), channel_id=1, replica_groups=mesh['section'=16,'expert'=8,'dp'=4] {'expert','dp'}, use_global_device_ids=true, to_apply=%region_1.0 | all-reduce | flops 128 | bytes 1024 | tf_op jit(solution)/shard_map/psum | solution.py:14
  72.2 0.8 fusion.22
  72.9 0.0 copy-start.3
  73.0 2.1 gather_fusion
  75.0 12.3 %all_to_all.10 = bf16[8,48,192]{2,1,0:T(8,128)(2,1)S(1)} all-to-all(bf16[8,48,192]{2,1,0:T(8,128)(2,1)S(1)} %bitcast.44), channel_id=1, replica_groups=mesh['section'=16,'expert'=8,'dp'=4] {'expert'}, dimensions={0} | all-to-all | bytes 294912 | tf_op jit(solution)/shard_map/all_to_all | solution.py:31
  87.4 0.1 copy.25
  87.4 0.8 reshape.68
  88.3 0.0 all-gather.2.cloned.1.call-update
  88.3 0.0 all-reduce.3.cloned.1.call-start
  88.3 88.4 %all-gather.2.cloned.1.call-done = bf16[768,1536]{1,0:T(8,128)(2,1)} async-done(((bf16[48,1536]{1,0:T(8,128)(2,1)}), bf16[768,1536]{1,0:T(8,128)(2,1)}) %all-gather.2.cloned.1.call-update) | async-done | bytes 2359312 | tf_op jit(solution)/shard_map/all_gather | solution.py:34
  176.7 0.0 copy-done.3
  176.7 0.0 copy-start.2
  176.7 0.0 copy-start.4
  176.7 3.2 fusion.12
  179.9 0.0 copy-done.2
  179.9 0.0 copy-done.4
  179.9 1.4 fusion.15
  181.3 1.3 pad_maximum_fusion
  182.6 0.0 all-reduce.3.cloned.1.call-update
  182.6 0.0 reduce-scatter.2.cloned.1.call-start
  182.6 60.4 %all-reduce.3.cloned.1.call-done = bf16[768,2,512]{2,0,1:T(8,128)(2,1)} async-done(((bf16[768,2,512]{2,0,1:T(8,128)(2,1)}), bf16[768,2,512]{2,0,1:T(8,128)(2,1)}) %all-reduce.3.cloned.1.call-update) | async-done | bytes 1572880 | tf_op jit(solution)/shard_map/psum | solution.py:38
  243.0 1.8 convert_element_type.40
  244.9 0.0 copy-done
  244.9 2.8 convolution_convert_fusion
  247.7 0.0 copy-start.1
  247.7 0.0 reduce-scatter.2.cloned.1.call-update
  247.8 213.0 %reduce-scatter.2.cloned.1.call-done = bf16[48,1536]{1,0:T(8,128)(2,1)} async-done(((bf16[768,1536]{1,0:T(8,128)(2,1)}), bf16[48,1536]{1,0:T(8,128)(2,1)}) %reduce-scatter.2.cloned.1.call-update) | async-done | bytes 147472 | tf_op jit(solution)/shard_map/reduce_scatter | solution.py:40
  460.7 1.1 reshape.69
  461.8 0.7 copy.29
  462.5 7.1 %all-to-all-start.1 = ((bf16[8,48,192]{2,1,0:T(8,128)(2,1)}), bf16[8,48,192]{2,1,0:T(8,128)(2,1)S(1)}, u32[]{:S(2)}, u32[]{:S(2)}) async-start(bf16[8,48,192]{2,1,0:T(8,128)(2,1)} %bitcast.41), calls=%async_computation.2 | async-start | bytes 393216 | tf_op jit(solution)/shard_map/all_to_all | solution.py:47
  469.7 0.0 copy-done.1
  469.7 0.1 copy.21
  469.8 8.5 %all-to-all-done.1 = bf16[8,48,192]{2,1,0:T(8,128)(2,1)S(1)} async-done(((bf16[8,48,192]{2,1,0:T(8,128)(2,1)}), bf16[8,48,192]{2,1,0:T(8,128)(2,1)S(1)}, u32[]{:S(2)}, u32[]{:S(2)}) %all-to-all-start.1) | async-done | bytes 147488 | tf_op jit(solution)/shard_map/all_to_all | solution.py:47
  478.3 1.2 gather_fusion.1
  479.4 0.1 reshape.71
  479.6 0.4 multiply_reduce_fusion
  480.0 0.7 copy.27
  (11 shorter events, 0.1 us)
Async XLA Ops:
  6.5 238.3 %copy-start = (bf16[1,512,1536]{2,1,0:T(8,128)(2,1)S(1)}, bf16[1,512,1536]{2,1,0:T(8,128)(2,1)}, u32[]{:S(2)}) copy-start(bf16[1,512,1536]{2,1,0:T(8,128)(2,1)} %param.13) | copy-start | bytes 4718596
  6.5 170.2 %all-gather.2.cloned.1.call-start = ((), (), s32[]{:S(2)}) async-start(), calls=%async_computation.3 | async-start | bytes 2506752 | tf_op jit(solution)/shard_map/all_gather | solution.py:34
  72.9 103.8 %copy-start.3 = (bf16[1,1536,512]{2,1,0:T(8,128)(2,1)S(1)}, bf16[1,1536,512]{2,1,0:T(8,128)(2,1)}, u32[]{:S(2)}) copy-start(bf16[1,1536,512]{2,1,0:T(8,128)(2,1)} %param.12) | copy-start | bytes 4718596
  88.3 154.8 %all-reduce.3.cloned.1.call-start = ((), (), s32[]{:S(2)}) async-start(), calls=%async_computation.4 | async-start | bytes 3145728 | tf_op jit(solution)/shard_map/psum | solution.py:38
  176.7 3.2 copy-start.2
  176.7 3.2 copy-start.4
  182.6 278.1 %reduce-scatter.2.cloned.1.call-start = ((), (), s32[]{:S(2)}) async-start(), calls=%async_computation.5 | async-start | bytes 2506752 | tf_op jit(solution)/shard_map/reduce_scatter | solution.py:40
  247.7 221.9 %copy-start.1 = (f32[128,2]{0,1:T(2,128)S(1)}, f32[128,2]{0,1:T(2,128)}, u32[]{:S(2)}) copy-start(f32[128,2]{0,1:T(2,128)} %param.10) | copy-start | bytes 3076
  462.5 15.8 %all-to-all-start.1 = ((bf16[8,48,192]{2,1,0:T(8,128)(2,1)}), bf16[8,48,192]{2,1,0:T(8,128)(2,1)S(1)}, u32[]{:S(2)}, u32[]{:S(2)}) async-start(bf16[8,48,192]{2,1,0:T(8,128)(2,1)} %bitcast.41), calls=%async_computation.2 | async-start | bytes 393216 | tf_op jit(solution)/shard_map/all_to_all | solution.py:47
Sparse Core Ops, SparseCore 0:
  88.4 88.2 all-gather.1
  182.7 60.2 all-reduce.2
  247.9 212.7 reduce-scatter.1
where the time goes:
time: 492 us; the launch traced here: 487 us
  waiting for transfers between devices  370 us (75%)
  blocking collectives  72.4 us (15%)
  between operations  13.3 us (3%)
  local copies, waits for them, and re-layouts  10.9 us (2%)
  matrix products  7.4 us (2%)
  starting transfers between devices  7.21 us (1%)
  other arithmetic  5.83 us (1%)
    reduce_scatter x1, waiting for transfers between devices, local(): lax.psum_scatter(jnp.dot(hidden, down_here, preferred_element_type=jnp.fl...  213 us
    all_gather x1, waiting for transfers between devices, local(): piece = lax.all_gather(joined, 'section', axis=0, tiled=True)  88.4 us
    psum x1, waiting for transfers between devices, local(): summed = lax.psum(paired.astype(jnp.bfloat16), 'dp').astype(jnp.float32)  60.4 us
    psum x1, blocking collectives, local(): squares = lax.psum(jnp.sum(stream * stream, axis=-1), ('expert', 'dp'))  60.1 us
    all_to_all x1, blocking collectives, local(): lax.all_to_all(picked, 'expert', split_axis=0, concat_axis=0, tiled=True)  12.3 us
  transfers between devices with their start and end apart: 4, of which 4 were waited for; matrix products, arithmetic and copies ran while one was open for 0% of the time, Pallas kernels for 0%

commit v1 on v0

v1 whole, which is shorter than its diff:
```python
import functools

import jax
import jax.numpy as jnp
from jax import lax
from jax.experimental import pallas as pl
from jax.experimental.pallas import tpu as pltpu
from jax.sharding import PartitionSpec as P

D = 6144
EPS = 1e-05
N_X = 2
F32 = jnp.float32
BF16 = jnp.bfloat16
LANES = 128


def dot(a, b):
    return jnp.dot(a, b, preferred_element_type=F32)


def dot_last(a, b):
    return lax.dot_general(a, b, (((1,), (1,)), ((), ())), preferred_element_type=F32)


def dot_first(a, b):
    return lax.dot_general(a, b, (((0,), (0,)), ((), ())), preferred_element_type=F32)


def split3(v):
    high = v.astype(BF16).astype(F32)
    rest = v - high
    mid = rest.astype(BF16).astype(F32)
    return high, mid, rest - mid


def pack(rows):
    cap = rows.shape[0]
    half = cap // 2
    tail = rows[:, LANES:]
    below = jnp.concatenate([tail[:half], tail[half:]], axis=1)
    pad = -half % 16
    if pad:
        below = jnp.concatenate([below, jnp.zeros((pad, LANES), F32)], axis=0)
    return rows[:, :LANES], below


def kernel(
    sizes,
    tok_ref,
    gain_ref,
    routes_ref,
    gates_ref,
    wg_hbm,
    wu_hbm,
    wd_hbm,
    out_ref,
    wg,
    wu,
    wd,
    w_sem,
    mix_top,
    mix_low,
    go,
    got,
    ss_out,
    ss_in,
    ag,
    part_out,
    part_in,
    hid,
    rs_out,
    rs_in,
    own,
    xr_out,
    xr_in,
    bk_out,
    bk_in,
    go_s,
    go_r,
    ss_s,
    ss_r,
    x_s,
    x_r,
    ag_s,
    ag_r,
    part_s,
    part_r,
    hid_s,
    hid_r,
    rs_s,
    rs_r,
    xr_s,
    xr_r,
    bk_s,
    bk_r,
):
    n_y, n_e, n_d, cap = sizes
    half = cap // 2
    low = half + (-half % 16)
    n_tok = tok_ref.shape[1]
    n_feat = tok_ref.shape[0]
    width = n_feat * n_e
    rows = N_X * cap
    sec = lax.axis_index("section")
    z = lax.axis_index("expert")
    d = lax.axis_index("dp")
    xh = lax.div(sec, n_y)
    y = lax.rem(sec, n_y)
    up = xh * n_y + lax.rem(y + 1, n_y)
    down = xh * n_y + lax.rem(y + n_y - 1, n_y)
    across = (1 - xh) * n_y + y

    def ring(h):
        return xh * n_y + lax.rem(y + 1 + h * (n_y - 2), n_y)

    def remote(src, dst, send, recv, **where):
        return pltpu.make_async_remote_copy(
            src_ref=src,
            dst_ref=dst,
            send_sem=send,
            recv_sem=recv,
            device_id=where,
            device_id_type=pl.DeviceIdType.MESH,
        )

    loads = [
        pltpu.make_async_copy(src.at[0], dst, w_sem.at[i])
        for i, (src, dst) in enumerate(((wg_hbm, wg), (wu_hbm, wu), (wd_hbm, wd)))
    ]
    for load in loads:
        load.start()

    barrier = pltpu.get_barrier_semaphore()
    for i in range(1, n_e):
        pl.semaphore_signal(barrier, inc=1, device_id={"expert": lax.rem(z + i, n_e)}, device_id_type=pl.DeviceIdType.MESH)
    for i in range(1, n_d):
        pl.semaphore_signal(barrier, inc=1, device_id={"dp": lax.rem(d + i, n_d)}, device_id_type=pl.DeviceIdType.MESH)
    for to in (up, down, across):
        pl.semaphore_signal(barrier, inc=1, device_id={"section": to}, device_id_type=pl.DeviceIdType.MESH)

    first = routes_ref[0:1, :]
    second = routes_ref[1:2, :]
    expert_ids = lax.broadcasted_iota(jnp.int32, (n_e, n_tok), 0)
    named = (first == expert_ids) | (second == expert_ids)
    earlier = (
        lax.broadcasted_iota(jnp.int32, (n_tok, n_tok), 0) < lax.broadcasted_iota(jnp.int32, (n_tok, n_tok), 1)
    )
    count = dot(jnp.where(named, 1.0, 0.0).astype(BF16), jnp.where(earlier, 1.0, 0.0).astype(BF16))
    slot = jnp.where(named, count, -1.0)
    weight = jnp.where(first == expert_ids, gates_ref[0:1, :], gates_ref[1:2, :])
    number = lax.broadcasted_iota(jnp.int32, (cap, n_tok), 0).astype(F32)
    low_row = lax.broadcasted_iota(jnp.int32, (low, n_tok), 0)
    low_number = jnp.where(low_row < half, low_row, 4 * cap).astype(F32)
    tops, lows, lows_more = [], [], []
    for e in range(n_e):
        mine = slot[e : e + 1, :]
        w = weight[e : e + 1, :]
        top = jnp.where(mine == number, 1.0, 0.0)
        low_a = jnp.where(mine == low_number, 1.0, 0.0)
        low_b = jnp.where(mine == low_number + half, 1.0, 0.0)
        tops.append(top.astype(BF16))
        lows.append(low_a.astype(BF16))
        lows_more.append(low_b.astype(BF16))
        for at, (part, store, size) in enumerate(((top, mix_top, cap), (low_a, mix_low, low), (low_b, mix_low, low))):
            lead = 0 if at == 0 else 2 * (at - 1)
            value = part * w
            high = value.astype(BF16)
            store[lead, e * size : (e + 1) * size, :] = high
            store[lead + 1, e * size : (e + 1) * size, :] = (value - high.astype(F32)).astype(BF16)
    tok = tok_ref[...]
    tail = tok[LANES:]
    blank = jnp.zeros_like(tail)
    sent_top = dot_last(jnp.concatenate(tops, axis=0), tok[:LANES])
    sent_low = dot_last(jnp.concatenate(lows, axis=0), jnp.concatenate([tail, blank], axis=0)) + dot_last(
        jnp.concatenate(lows_more, axis=0), jnp.concatenate([blank, tail], axis=0)
    )
    gain = gain_ref[...]
    gain_rows = list(split3(gain[:, :LANES])) + [
        jnp.concatenate([v, jnp.zeros((1, 2 * LANES - n_feat), F32)], axis=1) for v in split3(gain[:, LANES:])
    ]
    gain_block = jnp.concatenate(gain_rows + [jnp.zeros((2, LANES), F32)], axis=0)
    go[:, 0:cap, :] = sent_top.astype(BF16).reshape(n_e, cap, LANES)
    for e in range(n_e):
        block = sent_low[e * low : (e + 1) * low]
        go[e, cap : cap + low, :] = jnp.concatenate([block[:half], gain_block], axis=0).astype(BF16)

    pl.semaphore_wait(barrier, n_e - 1 + n_d - 1 + 3)

    def z_copy(src, dst, send, recv, i, outgoing):
        to = lax.rem(z + i, n_e)
        at = z if outgoing else to
        return remote(src.at[to], dst.at[at], send.at[i - 1], recv.at[at], expert=to)

    order = sorted(range(1, n_e), key=lambda i: -min(i, n_e - i))
    for i in order:
        z_copy(go, got, go_s, go_r, i, True).start()
    got[z] = go[z]
    for i in order[::-1]:
        z_copy(go, got, go_s, go_r, i, False).wait_recv()

    pieces, gains = [], []
    for e in range(n_e):
        block = got[e].astype(F32)
        below = block[cap : cap + half]
        edge = n_feat - LANES
        pieces.append(
            jnp.concatenate(
                [block[:cap], jnp.concatenate([below[:, :edge], below[:, edge : 2 * edge]], axis=0)], axis=1
            )
        )
        g = block[cap + half : cap + half + 8]
        gains.append(g[0:1] + g[1:2] + g[2:3])
        gains.append((g[3:4] + g[4:5] + g[5:6])[:, :edge])
    arrived = jnp.concatenate(pieces, axis=1)
    gain_all = jnp.concatenate(gains, axis=1)
    squares = jnp.sum(arrived * arrived, axis=1, keepdims=True)
    eye = lax.broadcasted_iota(jnp.int32, (cap, LANES), 0) == lax.broadcasted_iota(jnp.int32, (cap, LANES), 1)
    ss_out[...] = jnp.broadcast_to(jnp.sum(jnp.where(eye, squares, 0.0), axis=0, keepdims=True), ss_out.shape)

    def d_copy(src, dst, send, recv, i, outgoing):
        to = lax.rem(d + i, n_d)
        at = d if outgoing else to
        return remote(src, dst.at[at], send.at[i - 1], recv.at[at], dp=to)

    for i in range(1, n_d):
        d_copy(ss_out, ss_in, ss_s, ss_r, i, True).start()
    for i in range(1, n_d):
        d_copy(ss_out, ss_in, ss_s, ss_r, i, False).wait_recv()
    total = ss_out[0:1, :]
    for i in range(1, n_d):
        total = total + ss_in[lax.rem(d + i, n_d)][0:1, :]
    sums = jnp.sum(jnp.where(eye, total, 0.0), axis=1, keepdims=True)
    scale = lax.rsqrt(sums / (n_d * width) + EPS)
    ag[0, xh] = (arrived * scale * gain_all).astype(BF16)

    def ag_copy(b, h):
        return remote(ag.at[b, h], ag.at[b + 1, h], ag_s.at[b, h], ag_r.at[b + 1, h], section=ring(h))

    def ag_wait(b, h):
        remote(ag.at[b, h], ag.at[b, h], ag_s.at[b, h], ag_r.at[b, h], section=ring(h)).wait_recv()

    x_copy = remote(ag.at[0, xh], ag.at[0, xh], x_s, x_r, section=across)
    x_copy.start()
    ag_copy(0, xh).start()
    remote(ag.at[0, 1 - xh], ag.at[0, 1 - xh], x_s, x_r, section=across).wait_recv()
    ag_copy(0, 1 - xh).start()
    for load in loads:
        load.wait()

    def part_copy(b, i, outgoing):
        to = lax.rem(d + i, n_d)
        if outgoing:
            return remote(part_out.at[b, to], part_in.at[b, d], part_s.at[b, i - 1], part_r.at[b, d], dp=to)
        return remote(part_out.at[b, to], part_in.at[b, to], part_s.at[b, i - 1], part_r.at[b, to], dp=to)

    def hid_copy(b, i, outgoing):
        to = lax.rem(d + i, n_d)
        at = d if outgoing else to
        return remote(hid.at[b, d], hid.at[b, at], hid_s.at[b, i - 1], hid_r.at[b, at], dp=to)

    def rs_copy(b, h):
        return remote(rs_out.at[b, h], rs_in.at[b + 1, h], rs_s.at[b, h], rs_r.at[b + 1, h], section=ring(h))

    def rs_wait(b, h):
        remote(rs_in.at[b, h], rs_in.at[b, h], rs_s.at[0, h], rs_r.at[b, h], section=ring(h)).wait_recv()

    unit = wg.shape[1] // n_d

    def tick(t, carry):
        @pl.when(t < n_y)
        def _():
            @pl.when(t > 0)
            def _():
                for h in range(N_X):
                    ag_wait(t, h)

                    @pl.when(t < n_y - 1)
                    def _():
                        ag_copy(t, h).start()

            block = ag[t].reshape(rows, width)
            gate = dot(block, wg[...]).astype(BF16)
            upper = dot(block, wu[...]).astype(BF16)
            for p in range(n_d):
                part_out[t, p, :, 0:unit] = gate[:, p * unit : (p + 1) * unit]
                part_out[t, p, :, unit : 2 * unit] = upper[:, p * unit : (p + 1) * unit]
            for i in range(1, n_d):
                part_copy(t, i, True).start()

        @pl.when((t > 0) & (t < n_y + 1))
        def _():
            b = t - 1
            both = part_out[b, d].astype(F32)
            for i in range(1, n_d):
                part_copy(b, i, False).wait_recv()
                both = both + part_in[b, lax.rem(d + i, n_d)].astype(F32)
            g = both[:, 0:unit]
            hid[b, d] = (g / (1.0 + jnp.exp(-g)) * both[:, unit : 2 * unit]).astype(BF16)
            for i in range(1, n_d):
                hid_copy(b, i, True).start()

        @pl.when(t > 1)
        def _():
            b = t - 2
            for i in range(1, n_d):
                hid_copy(b, i, False).wait_recv()
            hidden = jnp.concatenate([hid[b, p] for p in range(n_d)], axis=1)
            result = dot(hidden, wd[...]).reshape(N_X, cap, width)

            @pl.when(b == 0)
            def _():
                own[...] = result

            @pl.when(b > 0)
            def _():
                for h in range(N_X):

                    @pl.when(b == 1)
                    def _():
                        rs_out[b, h] = result[h].astype(BF16)

                    @pl.when(b > 1)
                    def _():
                        rs_wait(b, h)
                        rs_out[b, h] = (result[h] + rs_in[b, h].astype(F32)).astype(BF16)

                    rs_copy(b, h).start()

        return carry

    lax.fori_loop(0, n_y + 2, tick, 0)

    other = 1 - xh
    rs_wait(n_y, other)
    xr_out[...] = (own[other] + rs_in[n_y, other].astype(F32)).astype(BF16)
    xr_copy = remote(xr_out, xr_in, xr_s, xr_r, section=across)
    xr_copy.start()
    rs_wait(n_y, xh)
    answer = own[xh] + rs_in[n_y, xh].astype(F32)
    xr_copy.wait_recv()
    answer = answer + xr_in[...].astype(F32)
    for e in range(n_e):
        top, below = pack(answer[:, e * n_feat : (e + 1) * n_feat])
        bk_out[e, 0:cap, :] = top.astype(BF16)
        bk_out[e, cap : cap + low, :] = below.astype(BF16)
    for i in order:
        z_copy(bk_out, bk_in, bk_s, bk_r, i, True).start()
    bk_in[z] = bk_out[z]
    for i in order[::-1]:
        z_copy(bk_out, bk_in, bk_s, bk_r, i, False).wait_recv()
    back_top = bk_in[:, 0:cap, :].reshape(n_e * cap, LANES)
    back_low = bk_in[:, cap : cap + low, :].reshape(n_e * low, LANES)
    edge = n_feat - LANES
    out_ref[0:LANES, :] = (
        tok_ref[0:LANES, :].astype(F32) + dot_first(back_top, mix_top[0]) + dot_first(back_top, mix_top[1])
    ).astype(BF16)
    low_a = dot_first(back_low, mix_low[0]) + dot_first(back_low, mix_low[1])
    low_b = dot_first(back_low, mix_low[2]) + dot_first(back_low, mix_low[3])
    out_ref[LANES:n_feat, :] = (
        tok_ref[LANES:n_feat, :].astype(F32) + low_a[0:edge] + low_b[edge : 2 * edge]
    ).astype(BF16)

    for i in order:
        z_copy(go, got, go_s, go_r, i, True).wait_send()
        z_copy(bk_out, bk_in, bk_s, bk_r, i, True).wait_send()
    for i in range(1, n_d):
        d_copy(ss_out, ss_in, ss_s, ss_r, i, True).wait_send()
    x_copy.wait_send()
    xr_copy.wait_send()

    def finish(b, carry):
        for i in range(1, n_d):
            part_copy(b, i, True).wait_send()
            hid_copy(b, i, True).wait_send()
        for h in range(N_X):

            @pl.when(b < n_y - 1)
            def _():
                ag_copy(b, h).wait_send()

            @pl.when(b > 0)
            def _():
                rs_copy(b, h).wait_send()

        return carry

    lax.fori_loop(0, n_y, finish, 0)


def local(tokens, norm_gain, routes, gates, w_gate, w_up, w_down):
    n_tok, n_feat = tokens.shape
    n_e = lax.axis_size("expert")
    n_d = lax.axis_size("dp")
    n_y = lax.axis_size("section") // N_X
    cap = min(n_tok, max(2, 3 * n_tok // n_e))
    half = cap // 2
    low = half + (-half % 16)
    width = n_feat * n_e
    units = w_gate.shape[2]
    unit = units // n_d
    rows = N_X * cap
    dma = pltpu.SemaphoreType.DMA
    vmem = pl.BlockSpec(memory_space=pltpu.VMEM)
    far = pl.BlockSpec(memory_space=pl.ANY)
    scratch = [
        pltpu.VMEM((width, units), BF16),
        pltpu.VMEM((width, units), BF16),
        pltpu.VMEM((units, width), BF16),
        dma((3,)),
        pltpu.VMEM((2, n_e * cap, n_tok), BF16),
        pltpu.VMEM((4, n_e * low, n_tok), BF16),
        pltpu.VMEM((n_e, cap + low, LANES), BF16),
        pltpu.VMEM((n_e, cap + low, LANES), BF16),
        pltpu.VMEM((8, LANES), F32),
        pltpu.VMEM((n_d, 8, LANES), F32),
        pltpu.VMEM((n_y, N_X, cap, width), BF16),
        pltpu.VMEM((n_y, n_d, rows, 2 * unit), BF16),
        pltpu.VMEM((n_y, n_d, rows, 2 * unit), BF16),
        pltpu.VMEM((n_y, n_d, rows, unit), BF16),
        pltpu.VMEM((n_y, N_X, cap, width), BF16),
        pltpu.VMEM((n_y + 1, N_X, cap, width), BF16),
        pltpu.VMEM((N_X, cap, width), F32),
        pltpu.VMEM((cap, width), BF16),
        pltpu.VMEM((cap, width), BF16),
        pltpu.VMEM((n_e, cap + low, LANES), BF16),
        pltpu.VMEM((n_e, cap + low, LANES), BF16),
        dma((n_e,)),
        dma((n_e,)),
        dma((n_d,)),
        dma((n_d,)),
        dma,
        dma,
        dma((n_y, N_X)),
        dma((n_y, N_X)),
        dma((n_y, n_d)),
        dma((n_y, n_d)),
        dma((n_y, n_d)),
        dma((n_y, n_d)),
        dma((n_y, N_X)),
        dma((n_y + 1, N_X)),
        dma,
        dma,
        dma((n_e,)),
        dma((n_e,)),
    ]
    mixed = pl.pallas_call(
        functools.partial(kernel, (n_y, n_e, n_d, cap)),
        out_shape=jax.ShapeDtypeStruct((n_feat, n_tok), BF16),
        in_specs=[vmem] * 4 + [far] * 3,
        out_specs=vmem,
        scratch_shapes=scratch,
        compiler_params=pltpu.CompilerParams(
            collective_id=0, has_side_effects=True, vmem_limit_bytes=48 * 1024 * 1024
        ),
        name="moe_layer",
    )(tokens.T, norm_gain.reshape(1, n_feat), routes.T, gates.T, w_gate, w_up, w_down)
    return mixed.T


def solution(mesh):
    in_specs = (
        P("section", ("dp", "expert")),
        P(("dp", "expert")),
        P("section", None),
        P("section", None),
        P("expert", "dp", "section"),
        P("expert", "dp", "section"),
        P("expert", "section", "dp"),
    )
    out_specs = P("section", ("dp", "expert"))
    return jax.shard_map(local, mesh=mesh, in_specs=in_specs, out_specs=out_specs, check_vma=False)
```

time: 492 us -> 105 us (0.21)
  waiting for transfers between devices: 370 us -> 0 us
  Pallas kernels: 0 us -> 95.3 us
  blocking collectives: 72.4 us -> 0 us
  between operations: 13.3 us -> 0.02 us
  matrix products: 7.4 us -> 0 us
  starting transfers between devices: 7.21 us -> 0 us
  other arithmetic: 5.83 us -> 0 us
    reduce_scatter x1 -> x0, waiting for transfers between devices: 213 us -> none  [local(): lax.psum_scatter(jnp.dot(hidden, down_here, preferred_element_type=jnp.fl...]
    pallas_call x0 -> x1, Pallas kernels: none -> 95.3 us  [local(): pl.pallas_call(functools.partial(kernel, (n_y, n_e, n_d, cap)), out_shape...]
    all_gather x1 -> x0, waiting for transfers between devices: 88.4 us -> none  [local(): piece = lax.all_gather(joined, 'section', axis=0, tiled=True)]
    psum x1 -> x0, waiting for transfers between devices: 60.4 us -> none  [local(): summed = lax.psum(paired.astype(jnp.bfloat16), 'dp').astype(jnp.float32)]
    psum x1 -> x0, blocking collectives: 60.1 us -> none  [local(): squares = lax.psum(jnp.sum(stream * stream, axis=-1), ('expert', 'dp'))]
    all_to_all x1 -> x0, blocking collectives: 12.3 us -> none  [local(): lax.all_to_all(picked, 'expert', split_axis=0, concat_axis=0, tiled=True)]
    all_to_all x1 -> x0, waiting for transfers between devices: 8.5 us -> none  [local(): lax.all_to_all(answer, 'expert', split_axis=0, concat_axis=0, tiled=True)]
    dot_general x3 -> x0, matrix products: 7.4 us -> none  [the longest x1 3.19 us: local(): up_part = jnp.dot(piece, up_here, preferred_element_type=jnp.float32)]
  transfers between devices with their start and end apart: 4 -> 0, of which waited for: 4 -> 0; matrix products, arithmetic and copies ran while one was open for 0% -> 0% of each run, Pallas kernels for 0% -> 0%
where the time goes in v1:
time: 105 us; the launch traced here: 103 us
  Pallas kernels  95.3 us (91%)
  local copies, waits for them, and re-layouts  7.68 us (7%)
    pallas_call x1, Pallas kernels, local(): pl.pallas_call(functools.partial(kernel, (n_y, n_e, n_d, cap)), out_shape...  95.3 us
    unnamed x15, local copies, waits for them, and re-layouts  7.68 us

profile of v1, /device:TPU:1, one launch (start us, length us, event | category | flops | bytes accessed | tf_op | source)
XLA Modules:
  0.0 103.0 jit_solution(14669290299088829844)
XLA Ops:
  0.0 0.0 copy-start
  0.0 1.4 %copy-done = bf16[1,1536,512]{2,1,0:T(8,128)(2,1)S(1)} copy-done((bf16[1,1536,512]{2,1,0:T(8,128)(2,1)S(1)}, bf16[1,1536,512]{2,1,0:T(8,128)(2,1)}, u32[]{:S(2)}) %copy-start) | copy-done | bytes 1572888
  1.4 0.0 copy-start.1
  1.4 1.4 %copy-done.1 = bf16[1,1536,512]{2,1,0:T(8,128)(2,1)S(1)} copy-done((bf16[1,1536,512]{2,1,0:T(8,128)(2,1)S(1)}, bf16[1,1536,512]{2,1,0:T(8,128)(2,1)}, u32[]{:S(2)}) %copy-start.1) | copy-done | bytes 1572888
  2.8 0.0 copy-start.2
  2.8 1.4 %copy-done.2 = bf16[1,512,1536]{2,1,0:T(8,128)(2,1)S(1)} copy-done((bf16[1,512,1536]{2,1,0:T(8,128)(2,1)S(1)}, bf16[1,512,1536]{2,1,0:T(8,128)(2,1)}, u32[]{:S(2)}) %copy-start.2) | copy-done | bytes 1572888
  4.2 0.0 copy-start.3
  4.2 0.8 copy-done.3
  5.0 0.0 copy-start.4
  5.0 0.7 copy-done.4
  5.7 0.0 copy-start.5
  5.7 0.7 copy-done.5
  6.4 0.0 copy-start.6
  6.4 0.7 copy-done.6
  7.1 95.3 %moe_layer.1 = bf16[192,128]{1,0:T(8,128)(2,1)S(1)} custom-call(bf16[192,128]{1,0:T(8,128)(2,1)S(1)} %bitcast.6, f32[1,192]{1,0:T(1,128)S(1)} %bitcast.7, s32[2,128]{1,0:T(2,128)S(1)} %bitcast.8, f32[2,128]{1,0:T(2,128)S(1)} %bitcast.9, bf16[1,1536,512]{2,1,0:T(8,128)(2,1)S(1)} %copy-done, bf16[1,1536,512]{2,1,0:T(8,128)(2,1)S(1)} %copy-done.1, ...), custom_call_target="tpu_custom_call" | custom-call | tf_op jit(solution)/shard_map/moe_layer/pallas_call | solution.py:447
  102.4 0.6 copy.9
Async XLA Ops:
  0.0 1.4 %copy-start = (bf16[1,1536,512]{2,1,0:T(8,128)(2,1)S(1)}, bf16[1,1536,512]{2,1,0:T(8,128)(2,1)}, u32[]{:S(2)}) copy-start(bf16[1,1536,512]{2,1,0:T(8,128)(2,1)} %wg_hbm.1) | copy-start | bytes 4718596
  1.4 1.4 %copy-start.1 = (bf16[1,1536,512]{2,1,0:T(8,128)(2,1)S(1)}, bf16[1,1536,512]{2,1,0:T(8,128)(2,1)}, u32[]{:S(2)}) copy-start(bf16[1,1536,512]{2,1,0:T(8,128)(2,1)} %wu_hbm.1) | copy-start | bytes 4718596
  2.8 1.4 %copy-start.2 = (bf16[1,512,1536]{2,1,0:T(8,128)(2,1)S(1)}, bf16[1,512,1536]{2,1,0:T(8,128)(2,1)}, u32[]{:S(2)}) copy-start(bf16[1,512,1536]{2,1,0:T(8,128)(2,1)} %wd_hbm.1) | copy-start | bytes 4718596
  4.2 0.8 copy-start.3
  5.0 0.7 copy-start.4
  5.7 0.7 copy-start.5
  6.4 0.7 copy-start.6

commit v2 on v1

v2 whole, which is shorter than its diff:
```python
import functools

import jax
import jax.numpy as jnp
from jax import lax
from jax.experimental import pallas as pl
from jax.experimental.pallas import tpu as pltpu
from jax.sharding import PartitionSpec as P

D = 6144
EPS = 1e-05
N_X = 2
F32 = jnp.float32
BF16 = jnp.bfloat16
LANES = 128
CHUNKS = 4


def dot(a, b):
    return jnp.dot(a, b, preferred_element_type=F32)


def dot_last(a, b):
    return lax.dot_general(a, b, (((1,), (1,)), ((), ())), preferred_element_type=F32)


def dot_first(a, b):
    return lax.dot_general(a, b, (((0,), (0,)), ((), ())), preferred_element_type=F32)


def split3(v):
    high = v.astype(BF16).astype(F32)
    rest = v - high
    mid = rest.astype(BF16).astype(F32)
    return high, mid, rest - mid


def pack(rows):
    half = rows.shape[0] // 2
    tail = rows[:, LANES:]
    return rows[:, :LANES], jnp.concatenate([tail[:half], tail[half:]], axis=1)


def kernel(
    sizes,
    tok_hbm,
    gain_hbm,
    routes_hbm,
    gates_hbm,
    wg_hbm,
    wu_hbm,
    wd_hbm,
    out_ref,
    tok_ref,
    gain_ref,
    routes_ref,
    gates_ref,
    wg,
    wu,
    wd,
    w_sem,
    mix_top,
    mix_low,
    go,
    got,
    ss_out,
    ss_in,
    sc,
    ag,
    part_out,
    part_in,
    hid,
    rs_out,
    rs_in,
    own,
    res,
    xr_out,
    xr_in,
    bk_out,
    bk_in,
    go_s,
    go_r,
    ss_s,
    ss_r,
    sx_s,
    sx_r,
    sc_s,
    sc_r,
    x_s,
    x_r,
    ag_s,
    ag_r,
    part_s,
    part_r,
    hid_s,
    hid_r,
    rs_s,
    rs_r,
    xr_s,
    xr_r,
    bk_s,
    bk_r,
):
    n_y, n_e, n_d, cap, n_c = sizes
    half = cap // 2
    low = half + 8
    n_feat, n_tok = tok_ref.shape
    edge = n_feat - LANES
    width = n_feat * n_e
    wide = width // n_c
    per = n_e // n_c
    rows = N_X * cap
    sec = lax.axis_index("section")
    z = lax.axis_index("expert")
    d = lax.axis_index("dp")
    xh = lax.div(sec, n_y)
    y = lax.rem(sec, n_y)
    up = xh * n_y + lax.rem(y + 1, n_y)
    down = xh * n_y + lax.rem(y + n_y - 1, n_y)
    across = (1 - xh) * n_y + y
    mine = lax.div(z, per)
    spread = sorted(range(n_c), key=lambda i: min(i, n_c - i))
    near_first = [lax.rem(mine + i, n_c) for i in spread]
    far_first = near_first[::-1]

    def ring(h):
        return xh * n_y + lax.rem(y + 1 + h * (n_y - 2), n_y)

    def remote(src, dst, send, recv, **where):
        return pltpu.make_async_remote_copy(
            src_ref=src,
            dst_ref=dst,
            send_sem=send,
            recv_sem=recv,
            device_id=where,
            device_id_type=pl.DeviceIdType.MESH,
        )

    barrier = pltpu.get_barrier_semaphore()

    def greet(**where):
        pl.semaphore_signal(barrier, inc=1, device_id=where, device_id_type=pl.DeviceIdType.MESH)

    order = sorted(range(1, n_e), key=lambda i: -min(i, n_e - i))
    for i in order:
        greet(expert=lax.rem(z + i, n_e))
    for to in (across, up, down):
        greet(section=to)
    for i in range(1, n_d):
        greet(dp=lax.rem(d + i, n_d))

    small = [
        pltpu.make_async_copy(src, dst, w_sem.at[i])
        for i, (src, dst) in enumerate(
            ((routes_hbm, routes_ref), (gates_hbm, gates_ref), (tok_hbm, tok_ref), (gain_hbm, gain_ref))
        )
    ]
    loads = [
        pltpu.make_async_copy(src.at[0], dst, w_sem.at[4 + i])
        for i, (src, dst) in enumerate(((wg_hbm, wg), (wu_hbm, wu), (wd_hbm, wd)))
    ]
    for load in small + loads:
        load.start()
    for load in small:
        load.wait()

    first = routes_ref[0:1, :]
    second = routes_ref[1:2, :]
    expert_ids = lax.broadcasted_iota(jnp.int32, (n_e, n_tok), 0)
    named = (first == expert_ids) | (second == expert_ids)
    earlier = (
        lax.broadcasted_iota(jnp.int32, (n_tok, n_tok), 0) < lax.broadcasted_iota(jnp.int32, (n_tok, n_tok), 1)
    )
    count = dot(jnp.where(named, 1.0, 0.0).astype(BF16), jnp.where(earlier, 1.0, 0.0).astype(BF16))
    slot = jnp.where(named, count, -1.0)
    weight = jnp.where(first == expert_ids, gates_ref[0:1, :], gates_ref[1:2, :])
    number = lax.broadcasted_iota(jnp.int32, (LANES, n_tok), 0).astype(F32)
    low_row = lax.broadcasted_iota(jnp.int32, (low, n_tok), 0)
    low_number = jnp.where(low_row < half, low_row, 4 * cap).astype(F32)
    picks = [jnp.where(slot[e : e + 1, :] == number, 1.0, 0.0) for e in range(n_e)]
    lows_a = [jnp.where(slot[e : e + 1, :] == low_number, 1.0, 0.0) for e in range(n_e)]
    lows_b = [jnp.where(slot[e : e + 1, :] == low_number + half, 1.0, 0.0) for e in range(n_e)]

    def stacked(parts):
        return jnp.concatenate([part.astype(BF16) for part in parts], axis=0)

    tok = tok_ref[...]
    tail = tok[LANES:]
    blank = jnp.zeros_like(tail)
    gain = gain_ref[...]
    gain_tail = gain[:, LANES:]
    sent_top = dot_last(stacked([p[:cap] for p in picks]), tok[:LANES]) * gain[:, :LANES]
    sent_low = (
        dot_last(stacked(lows_a), jnp.concatenate([tail, blank], axis=0))
        + dot_last(stacked(lows_b), jnp.concatenate([blank, tail], axis=0))
    ) * jnp.concatenate([gain_tail, gain_tail], axis=1)
    tok32 = tok.astype(F32)
    squares = split3(jnp.sum(tok32 * tok32, axis=0, keepdims=True))
    squares = jnp.concatenate(list(squares) + [jnp.zeros((5, n_tok), F32)], axis=0).astype(BF16)
    sent_squares = dot_last(squares, stacked(picks))
    go[:, 0:cap, :] = sent_top.astype(BF16).reshape(n_e, cap, LANES)
    for e in range(n_e):
        go[e, cap : cap + low, :] = jnp.concatenate(
            [sent_low[e * low : e * low + half], sent_squares[:, e * LANES : (e + 1) * LANES]], axis=0
        ).astype(BF16)

    pl.semaphore_wait(barrier, n_e - 1 + n_d - 1 + 3)

    def z_copy(src, dst, send, recv, i, outgoing):
        to = lax.rem(z + i, n_e)
        at = z if outgoing else to
        return remote(src.at[to], dst.at[at], send.at[to], recv.at[at], expert=to)

    for i in order:
        z_copy(go, got, go_s, go_r, i, True).start()
    got[z] = go[z]

    def x_copy(c, outgoing):
        h = xh if outgoing else 1 - xh
        return remote(ag.at[0, h, c], ag.at[0, h, c], x_s.at[c], x_r.at[c], section=across)

    def ag_copy(b, h, c):
        return remote(ag.at[b, h, c], ag.at[b + 1, h, c], ag_s.at[b, h, c], ag_r.at[b + 1, h, c], section=ring(h))

    def ag_wait(b, h, c):
        remote(ag.at[b, h, c], ag.at[b, h, c], ag_s.at[b, h, c], ag_r.at[b, h, c], section=ring(h)).wait_recv()

    for e in range(n_e):
        w = weight[e : e + 1, :]
        for part, store, lead, size in (
            (picks[e][:cap], mix_top, 0, cap),
            (lows_a[e], mix_low, 0, low),
            (lows_b[e], mix_low, 2, low),
        ):
            value = part * w
            high = value.astype(BF16)
            store[lead, e * size : (e + 1) * size, :] = high
            store[lead + 1, e * size : (e + 1) * size, :] = (value - high.astype(F32)).astype(BF16)

    row_squares = jnp.zeros((1, LANES), F32)
    for c in near_first:
        pieces = []
        for k in range(per):
            zp = c * per + k

            @pl.when(zp != z)
            def _():
                remote(go.at[zp], got.at[zp], go_s.at[zp], go_r.at[zp], expert=zp).wait_recv()

            block = got[zp].astype(F32)
            below = block[cap : cap + half]
            pieces.append(
                jnp.concatenate(
                    [block[:cap], jnp.concatenate([below[:, :edge], below[:, edge : 2 * edge]], axis=0)], axis=1
                )
            )
            terms = block[cap + half : cap + half + 8]
            row_squares = row_squares + (terms[0:1] + terms[1:2] + terms[2:3])
        ag[0, xh, c] = jnp.concatenate(pieces, axis=1).astype(BF16)
        x_copy(c, True).start()
        ag_copy(0, xh, c).start()

    def d_copy(src, dst, send, recv, i, outgoing):
        to = lax.rem(d + i, n_d)
        at = d if outgoing else to
        return remote(src, dst.at[at], send.at[to], recv.at[at], dp=to)

    ss_out[...] = jnp.broadcast_to(row_squares, ss_out.shape)
    for i in range(1, n_d):
        d_copy(ss_out, ss_in, ss_s, ss_r, i, True).start()
    for c in near_first:
        x_copy(c, False).wait_recv()
        ag_copy(0, 1 - xh, c).start()
    total = row_squares
    for i in range(1, n_d):
        d_copy(ss_out, ss_in, ss_s, ss_r, i, False).wait_recv()
        total = total + ss_in[lax.rem(d + i, n_d)][0:1, :]
    sc[0, xh] = jnp.broadcast_to(lax.rsqrt(total / (n_d * width) + EPS), ss_out.shape)
    sx_copy = remote(sc.at[0, xh], sc.at[0, xh], sx_s, sx_r, section=across)
    sx_copy.start()
    for load in loads:
        load.wait()

    def sc_copy(b, h):
        return remote(sc.at[b, h], sc.at[b + 1, h], sc_s.at[b, h], sc_r.at[b + 1, h], section=ring(h))

    def part_copy(b, i, outgoing):
        to = lax.rem(d + i, n_d)
        at = d if outgoing else to
        return remote(part_out.at[b, to], part_in.at[b, at], part_s.at[b, to], part_r.at[b, at], dp=to)

    def hid_copy(b, i, outgoing):
        to = lax.rem(d + i, n_d)
        at = d if outgoing else to
        return remote(hid.at[b, d], hid.at[b, at], hid_s.at[b, to], hid_r.at[b, at], dp=to)

    def rs_copy(b, h, c):
        return remote(
            rs_out.at[b, h, c], rs_in.at[b + 1, h, c], rs_s.at[b, h, c], rs_r.at[b + 1, h, c], section=ring(h)
        )

    def rs_wait(b, h, c):
        remote(rs_in.at[b, h, c], rs_in.at[b, h, c], rs_s.at[0, h, c], rs_r.at[b, h, c], section=ring(h)).wait_recv()

    unit = wg.shape[1] // n_d
    eye = lax.broadcasted_iota(jnp.int32, (cap, LANES), 0) == lax.broadcasted_iota(jnp.int32, (cap, LANES), 1)

    def tick(t, carry):
        @pl.when(t < n_y)
        def _():
            @pl.when(t > 0)
            def _():
                for c in near_first:
                    for h in range(N_X):
                        ag_wait(t, h, c)

                        @pl.when(t < n_y - 1)
                        def _():
                            ag_copy(t, h, c).start()

            block = jnp.concatenate([ag[t, :, c].reshape(rows, wide) for c in range(n_c)], axis=1)
            gate = dot(block, wg[...]).astype(BF16)
            upper = dot(block, wu[...]).astype(BF16)
            for p in range(n_d):
                part_out[t, p, :, 0:unit] = gate[:, p * unit : (p + 1) * unit]
                part_out[t, p, :, unit : 2 * unit] = upper[:, p * unit : (p + 1) * unit]
            for i in range(1, n_d):
                part_copy(t, i, True).start()

        @pl.when((t > 0) & (t < n_y + 1))
        def _():
            b = t - 1

            @pl.when(b == 0)
            def _():
                remote(sc.at[0, 1 - xh], sc.at[0, 1 - xh], sx_s, sx_r, section=across).wait_recv()

            scales = []
            for h in range(N_X):

                @pl.when(b > 0)
                def _():
                    remote(sc.at[b, h], sc.at[b, h], sc_s.at[0, h], sc_r.at[b, h], section=ring(h)).wait_recv()

                @pl.when(b < n_y - 1)
                def _():
                    sc_copy(b, h).start()

                scales.append(jnp.sum(jnp.where(eye, sc[b, h][0:1, :], 0.0), axis=1, keepdims=True))
            both = part_out[b, d].astype(F32)
            for i in range(1, n_d):
                part_copy(b, i, False).wait_recv()
                both = both + part_in[b, lax.rem(d + i, n_d)].astype(F32)
            both = both * jnp.concatenate(scales, axis=0)
            g = both[:, 0:unit]
            hid[b, d] = (g / (1.0 + jnp.exp(-g)) * both[:, unit : 2 * unit]).astype(BF16)
            for i in range(1, n_d):
                hid_copy(b, i, True).start()

        @pl.when(t > 1)
        def _():
            b = t - 2
            for i in range(1, n_d):
                hid_copy(b, i, False).wait_recv()
            hidden = jnp.concatenate([hid[b, p] for p in range(n_d)], axis=1)
            result = dot(hidden, wd[...])

            def keep(ref):
                for h in range(N_X):
                    for c in range(n_c):
                        ref[h, c] = result[h * cap : (h + 1) * cap, c * wide : (c + 1) * wide]

            @pl.when(b == 0)
            def _():
                keep(own)

            @pl.when(b > 0)
            def _():
                keep(res)
                for c in far_first:
                    for h in range(N_X):

                        @pl.when(b == 1)
                        def _():
                            rs_out[b, h, c] = res[h, c].astype(BF16)

                        @pl.when(b > 1)
                        def _():
                            rs_wait(b, h, c)
                            rs_out[b, h, c] = (res[h, c] + rs_in[b, h, c].astype(F32)).astype(BF16)

                        rs_copy(b, h, c).start()

        return carry

    lax.fori_loop(0, n_y + 2, tick, 0)

    other = 1 - xh

    def xr_copy(c):
        return remote(xr_out.at[c], xr_in.at[c], xr_s.at[c], xr_r.at[c], section=across)

    for c in far_first:
        rs_wait(n_y, other, c)
        xr_out[c] = (own[other, c] + rs_in[n_y, other, c].astype(F32)).astype(BF16)
        xr_copy(c).start()
    for c in far_first:
        rs_wait(n_y, xh, c)
        answer = own[xh, c] + rs_in[n_y, xh, c].astype(F32)
        xr_copy(c).wait_recv()
        answer = answer + xr_in[c].astype(F32)
        for k in range(per):
            zp = c * per + k
            top, below = pack(answer[:, k * n_feat : (k + 1) * n_feat])
            bk_out[zp, 0:cap, :] = top.astype(BF16)
            bk_out[zp, cap : cap + low, :] = jnp.concatenate([below, jnp.zeros((8, LANES), F32)], axis=0).astype(BF16)

            @pl.when(zp != z)
            def _():
                remote(bk_out.at[zp], bk_in.at[z], bk_s.at[zp], bk_r.at[z], expert=zp).start()

    bk_in[z] = bk_out[z]
    for i in order[::-1]:
        z_copy(bk_out, bk_in, bk_s, bk_r, i, False).wait_recv()
    back_top = bk_in[:, 0:cap, :].reshape(n_e * cap, LANES)
    back_low = bk_in[:, cap : cap + low, :].reshape(n_e * low, LANES)
    out_ref[0:LANES, :] = (
        tok_ref[0:LANES, :].astype(F32) + dot_first(back_top, mix_top[0]) + dot_first(back_top, mix_top[1])
    ).astype(BF16)
    low_a = dot_first(back_low, mix_low[0]) + dot_first(back_low, mix_low[1])
    low_b = dot_first(back_low, mix_low[2]) + dot_first(back_low, mix_low[3])
    out_ref[LANES:n_feat, :] = (
        tok_ref[LANES:n_feat, :].astype(F32) + low_a[0:edge] + low_b[edge : 2 * edge]
    ).astype(BF16)

    for i in order:
        z_copy(go, got, go_s, go_r, i, True).wait_send()
        z_copy(bk_out, bk_in, bk_s, bk_r, i, True).wait_send()
    for i in range(1, n_d):
        d_copy(ss_out, ss_in, ss_s, ss_r, i, True).wait_send()
    sx_copy.wait_send()
    for c in range(n_c):
        x_copy(c, True).wait_send()
        xr_copy(c).wait_send()

    def finish(b, carry):
        for i in range(1, n_d):
            part_copy(b, i, True).wait_send()
            hid_copy(b, i, True).wait_send()
        for h in range(N_X):

            @pl.when(b < n_y - 1)
            def _():
                sc_copy(b, h).wait_send()
                for c in range(n_c):
                    ag_copy(b, h, c).wait_send()

            @pl.when(b > 0)
            def _():
                for c in range(n_c):
                    rs_copy(b, h, c).wait_send()

        return carry

    lax.fori_loop(0, n_y, finish, 0)


def local(tokens, norm_gain, routes, gates, w_gate, w_up, w_down):
    n_tok, n_feat = tokens.shape
    n_e = lax.axis_size("expert")
    n_d = lax.axis_size("dp")
    n_y = lax.axis_size("section") // N_X
    n_c = min(CHUNKS, n_e)
    cap = min(n_tok, max(2, 3 * n_tok // n_e))
    low = cap // 2 + 8
    width = n_feat * n_e
    wide = width // n_c
    units = w_gate.shape[2]
    unit = units // n_d
    rows = N_X * cap
    dma = pltpu.SemaphoreType.DMA
    far = pl.BlockSpec(memory_space=pl.ANY)
    scratch = [
        pltpu.VMEM((n_feat, n_tok), BF16),
        pltpu.VMEM((1, n_feat), F32),
        pltpu.VMEM((2, n_tok), jnp.int32),
        pltpu.VMEM((2, n_tok), F32),
        pltpu.VMEM((width, units), BF16),
        pltpu.VMEM((width, units), BF16),
        pltpu.VMEM((units, width), BF16),
        dma((7,)),
        pltpu.VMEM((2, n_e * cap, n_tok), BF16),
        pltpu.VMEM((4, n_e * low, n_tok), BF16),
        pltpu.VMEM((n_e, cap + low, LANES), BF16),
        pltpu.VMEM((n_e, cap + low, LANES), BF16),
        pltpu.VMEM((8, LANES), F32),
        pltpu.VMEM((n_d, 8, LANES), F32),
        pltpu.VMEM((n_y, N_X, 8, LANES), F32),
        pltpu.VMEM((n_y, N_X, n_c, cap, wide), BF16),
        pltpu.VMEM((n_y, n_d, rows, 2 * unit), BF16),
        pltpu.VMEM((n_y, n_d, rows, 2 * unit), BF16),
        pltpu.VMEM((n_y, n_d, rows, unit), BF16),
        pltpu.VMEM((n_y, N_X, n_c, cap, wide), BF16),
        pltpu.VMEM((n_y + 1, N_X, n_c, cap, wide), BF16),
        pltpu.VMEM((N_X, n_c, cap, wide), F32),
        pltpu.VMEM((N_X, n_c, cap, wide), F32),
        pltpu.VMEM((n_c, cap, wide), BF16),
        pltpu.VMEM((n_c, cap, wide), BF16),
        pltpu.VMEM((n_e, cap + low, LANES), BF16),
        pltpu.VMEM((n_e, cap + low, LANES), BF16),
        dma((n_e,)),
        dma((n_e,)),
        dma((n_d,)),
        dma((n_d,)),
        dma,
        dma,
        dma((n_y, N_X)),
        dma((n_y, N_X)),
        dma((n_c,)),
        dma((n_c,)),
        dma((n_y, N_X, n_c)),
        dma((n_y, N_X, n_c)),
        dma((n_y, n_d)),
        dma((n_y, n_d)),
        dma((n_y, n_d)),
        dma((n_y, n_d)),
        dma((n_y, N_X, n_c)),
        dma((n_y + 1, N_X, n_c)),
        dma((n_c,)),
        dma((n_c,)),
        dma((n_e,)),
        dma((n_e,)),
    ]
    mixed = pl.pallas_call(
        functools.partial(kernel, (n_y, n_e, n_d, cap, n_c)),
        out_shape=jax.ShapeDtypeStruct((n_feat, n_tok), BF16),
        in_specs=[far] * 7,
        out_specs=pl.BlockSpec(memory_space=pltpu.VMEM),
        scratch_shapes=scratch,
        compiler_params=pltpu.CompilerParams(
            collective_id=0, has_side_effects=True, vmem_limit_bytes=64 * 1024 * 1024
        ),
        name="moe_layer",
    )(tokens.T, norm_gain.reshape(1, n_feat), routes.T, gates.T, w_gate, w_up, w_down)
    return mixed.T


def solution(mesh):
    in_specs = (
        P("section", ("dp", "expert")),
        P(("dp", "expert")),
        P("section", None),
        P("section", None),
        P("expert", "dp", "section"),
        P("expert", "dp", "section"),
        P("expert", "section", "dp"),
    )
    out_specs = P("section", ("dp", "expert"))
    return jax.shard_map(local, mesh=mesh, in_specs=in_specs, out_specs=out_specs, check_vma=False)
```

time: 105 us -> 88.4 us (0.84); the launches traced: 103 us -> 87.5 us
  Pallas kernels: 95.3 us -> 86.1 us
  local copies, waits for them, and re-layouts: 7.68 us -> 1.42 us
    pallas_call x1, Pallas kernels: 95.3 us -> 86.1 us  [local(): pl.pallas_call(functools.partial(kernel, (n_y, n_e, n_d, cap, n_c)), out_...]
    unnamed x15 -> x1, local copies, waits for them, and re-layouts: 7.68 us -> 1.42 us
where the time goes in v2:
time: 88.4 us; the launch traced here: 87.5 us
  Pallas kernels  86.1 us (97%)
  local copies, waits for them, and re-layouts  1.42 us (2%)
    pallas_call x1, Pallas kernels, local(): pl.pallas_call(functools.partial(kernel, (n_y, n_e, n_d, cap, n_c)), out_...  86.1 us

profile of v2, /device:TPU:1, one launch (start us, length us, event | category | flops | bytes accessed | tf_op | source)
XLA Modules:
  0.0 87.5 jit_solution(10546191821946145776)
XLA Ops:
  0.0 86.1 %moe_layer.1 = bf16[192,128]{1,0:T(8,128)(2,1)} custom-call(bf16[192,128]{1,0:T(8,128)(2,1)} %bitcast.6, f32[1,192]{1,0:T(1,128)} %bitcast.7, s32[2,128]{1,0:T(2,128)} %bitcast.8, f32[2,128]{1,0:T(2,128)} %bitcast.9, bf16[1,1536,512]{2,1,0:T(8,128)(2,1)} %wg_hbm.1, bf16[1,1536,512]{2,1,0:T(8,128)(2,1)} %wu_hbm.1, bf16[1,512,1536]{2,1,0:T(8,128)(2,1)} %wd_hbm.1), custom_call_target="tpu_custom_call" | custom-call | tf_op jit(solution)/shard_map/moe_layer/pallas_call | solution.py:534
  86.1 1.4 %copy.9 = bf16[128,192]{0,1:T(8,128)(2,1)} copy(bf16[128,192]{0,1:T(8,128)(2,1)} %bitcast.5) | data formatting | bytes 98304

commit v3 on v2

v3 whole, which is shorter than its diff:
```python
import functools

import jax
import jax.numpy as jnp
from jax import lax
from jax.experimental import pallas as pl
from jax.experimental.pallas import tpu as pltpu
from jax.sharding import PartitionSpec as P

D = 6144
EPS = 1e-05
N_X = 2
F32 = jnp.float32
BF16 = jnp.bfloat16
LANES = 128
CHUNKS = 4
RING = 3
TURN = 4


def dot(a, b):
    return jnp.dot(a, b, preferred_element_type=F32)


def dot_last(a, b):
    return lax.dot_general(a, b, (((1,), (1,)), ((), ())), preferred_element_type=F32)


def dot_first(a, b):
    return lax.dot_general(a, b, (((0,), (0,)), ((), ())), preferred_element_type=F32)


def split3(v):
    high = v.astype(BF16).astype(F32)
    rest = v - high
    mid = rest.astype(BF16).astype(F32)
    return high, mid, rest - mid


def pack(rows):
    half = rows.shape[0] // 2
    tail = rows[:, LANES:]
    return rows[:, :LANES], jnp.concatenate([tail[:half], tail[half:]], axis=1)


def kernel(
    sizes,
    tok_hbm,
    gain_hbm,
    routes_hbm,
    gates_hbm,
    wg_hbm,
    wu_hbm,
    wd_hbm,
    out_ref,
    tok_ref,
    gain_ref,
    routes_ref,
    gates_ref,
    wg,
    wu,
    wd,
    w_sem,
    mix_top,
    mix_low,
    go,
    got,
    ss_out,
    ss_in,
    sc,
    ag,
    part_out,
    part_in,
    hid,
    hid_in,
    own,
    res,
    rs_out,
    rs_in,
    xr_out,
    xr_in,
    bk_out,
    bk_in,
    go_s,
    go_r,
    ss_s,
    ss_r,
    sx_s,
    sx_r,
    sc_s,
    sc_r,
    x_s,
    x_r,
    ag_s,
    ag_r,
    part_s,
    part_r,
    hid_s,
    hid_r,
    rs_s,
    rs_r,
    xr_s,
    xr_r,
    bk_s,
    bk_r,
):
    n_y, n_e, n_d, cap, n_c = sizes
    half = cap // 2
    low = half + 8
    n_feat, n_tok = tok_ref.shape
    edge = n_feat - LANES
    width = n_feat * n_e
    wide = width // n_c
    per = n_e // n_c
    rows = N_X * cap
    sec = lax.axis_index("section")
    z = lax.axis_index("expert")
    d = lax.axis_index("dp")
    xh = lax.div(sec, n_y)
    y = lax.rem(sec, n_y)
    up = xh * n_y + lax.rem(y + 1, n_y)
    down = xh * n_y + lax.rem(y + n_y - 1, n_y)
    across = (1 - xh) * n_y + y
    mine = lax.div(z, per)
    spread = sorted(range(n_c), key=lambda i: min(i, n_c - i))
    near_first = [lax.rem(mine + i, n_c) for i in spread]
    far_first = near_first[::-1]

    def ring(h):
        return xh * n_y + lax.rem(y + 1 + h * (n_y - 2), n_y)

    def remote(src, dst, send, recv, **where):
        return pltpu.make_async_remote_copy(
            src_ref=src,
            dst_ref=dst,
            send_sem=send,
            recv_sem=recv,
            device_id=where,
            device_id_type=pl.DeviceIdType.MESH,
        )

    barrier = pltpu.get_barrier_semaphore()

    def greet(**where):
        pl.semaphore_signal(barrier, inc=1, device_id=where, device_id_type=pl.DeviceIdType.MESH)

    order = sorted(range(1, n_e), key=lambda i: -min(i, n_e - i))
    for i in order:
        greet(expert=lax.rem(z + i, n_e))
    for to in (across, up, down):
        greet(section=to)
    for i in range(1, n_d):
        greet(dp=lax.rem(d + i, n_d))

    small = [
        pltpu.make_async_copy(src, dst, w_sem.at[i])
        for i, (src, dst) in enumerate(
            ((routes_hbm, routes_ref), (gates_hbm, gates_ref), (tok_hbm, tok_ref), (gain_hbm, gain_ref))
        )
    ]
    loads = [
        pltpu.make_async_copy(src.at[0], dst, w_sem.at[4 + i])
        for i, (src, dst) in enumerate(((wg_hbm, wg), (wu_hbm, wu), (wd_hbm, wd)))
    ]
    for load in small + loads:
        load.start()
    for load in small:
        load.wait()

    first = routes_ref[0:1, :]
    second = routes_ref[1:2, :]
    expert_ids = lax.broadcasted_iota(jnp.int32, (n_e, n_tok), 0)
    named = (first == expert_ids) | (second == expert_ids)
    earlier = (
        lax.broadcasted_iota(jnp.int32, (n_tok, n_tok), 0) < lax.broadcasted_iota(jnp.int32, (n_tok, n_tok), 1)
    )
    count = dot(jnp.where(named, 1.0, 0.0).astype(BF16), jnp.where(earlier, 1.0, 0.0).astype(BF16))
    slot = jnp.where(named, count, -1.0)
    weight = jnp.where(first == expert_ids, gates_ref[0:1, :], gates_ref[1:2, :])
    number = lax.broadcasted_iota(jnp.int32, (cap, n_tok), 0).astype(F32)
    picks = [jnp.where(slot[e : e + 1, :] == number, 1.0, 0.0) for e in range(n_e)]
    eye = lax.broadcasted_iota(jnp.int32, (cap, LANES), 0) == lax.broadcasted_iota(jnp.int32, (cap, LANES), 1)
    picked = dot_last(jnp.concatenate([p.astype(BF16) for p in picks], axis=0), tok_ref[...])
    squares = jnp.sum(picked * picked, axis=1, keepdims=True)
    picked = picked * gain_ref[...]
    for e in range(n_e):
        top, below = pack(picked[e * cap : (e + 1) * cap])
        go[e, 0:cap, :] = top.astype(BF16)
        terms = split3(jnp.sum(jnp.where(eye, squares[e * cap : (e + 1) * cap], 0.0), axis=0, keepdims=True))
        go[e, cap : cap + low, :] = jnp.concatenate(
            [below] + list(terms) + [jnp.zeros((5, LANES), F32)], axis=0
        ).astype(BF16)

    pl.semaphore_wait(barrier, n_e - 1 + n_d - 1 + 3)

    def z_copy(src, dst, send, recv, to):
        return remote(src.at[to], dst.at[z], send, recv, expert=to)

    for i in order:
        z_copy(go, got, go_s, go_r.at[z], lax.rem(z + i, n_e)).start()
    got[z] = go[z]

    def x_copy(c):
        return remote(ag.at[0, xh, c], ag.at[0, xh, c], x_s, x_r.at[c], section=across)

    def ag_copy(b, h, c):
        at = lax.rem(b, RING)
        return remote(
            ag.at[b, h, c], ag.at[b + 1, h, c], ag_s.at[at, h], ag_r.at[lax.rem(b + 1, RING), h, c], section=ring(h)
        )

    def ag_sent(b, h):
        remote(ag.at[b, h], ag.at[b, h], ag_s.at[lax.rem(b, RING), h], ag_r.at[0, h, 0], section=ring(h)).wait_send()

    def ag_wait(b, h, c):
        at = lax.rem(b, RING)
        remote(ag.at[b, h, c], ag.at[b, h, c], ag_s.at[at, h], ag_r.at[at, h, c], section=ring(h)).wait_recv()

    low_row = lax.broadcasted_iota(jnp.int32, (low, n_tok), 0)
    low_number = jnp.where(low_row < half, low_row, 4 * cap).astype(F32)
    for e in range(n_e):
        mark = slot[e : e + 1, :]
        w = weight[e : e + 1, :]
        for part, store, lead, size in (
            (picks[e], mix_top, 0, cap),
            (jnp.where(mark == low_number, 1.0, 0.0), mix_low, 0, low),
            (jnp.where(mark == low_number + half, 1.0, 0.0), mix_low, 2, low),
        ):
            value = part * w
            high = value.astype(BF16)
            store[lead, e * size : (e + 1) * size, :] = high
            store[lead + 1, e * size : (e + 1) * size, :] = (value - high.astype(F32)).astype(BF16)

    row_squares = jnp.zeros((1, LANES), F32)
    for c in near_first:
        pieces = []
        for k in range(per):
            zp = c * per + k

            @pl.when(zp != z)
            def _():
                remote(go.at[zp], got.at[zp], go_s, go_r.at[zp], expert=zp).wait_recv()

            block = got[zp].astype(F32)
            below = block[cap : cap + half]
            pieces.append(
                jnp.concatenate(
                    [block[:cap], jnp.concatenate([below[:, :edge], below[:, edge : 2 * edge]], axis=0)], axis=1
                )
            )
            terms = block[cap + half : cap + half + 8]
            row_squares = row_squares + (terms[0:1] + terms[1:2] + terms[2:3])
        ag[0, xh, c] = jnp.concatenate(pieces, axis=1).astype(BF16)
        x_copy(c).start()
        ag_copy(0, xh, c).start()

    def d_copy(src, dst, send, recv, i):
        return remote(src, dst.at[i - 1], send, recv, dp=lax.rem(d + i, n_d))

    def d_all(dst, send, recv):
        return remote(dst, dst, send, recv, dp=lax.rem(d + 1, n_d))

    ss_out[...] = jnp.broadcast_to(row_squares, ss_out.shape)
    for i in range(1, n_d):
        d_copy(ss_out, ss_in, ss_s, ss_r, i).start()
    for c in near_first:
        remote(ag.at[0, 1 - xh, c], ag.at[0, 1 - xh, c], x_s, x_r.at[c], section=across).wait_recv()
        ag_copy(0, 1 - xh, c).start()
    d_all(ss_in, ss_s, ss_r).wait_recv()
    total = row_squares
    for i in range(n_d - 1):
        total = total + ss_in[i][0:1, :]
    sc[0, xh] = jnp.broadcast_to(lax.rsqrt(total / (n_d * width) + EPS), ss_out.shape)
    sx_copy = remote(sc.at[0, xh], sc.at[0, xh], sx_s, sx_r, section=across)
    sx_copy.start()
    for load in loads:
        load.wait()

    def sc_copy(b, h):
        at = lax.rem(b, 2)
        return remote(sc.at[b, h], sc.at[b + 1, h], sc_s.at[at, h], sc_r.at[1 - at, h], section=ring(h))

    def part_copy(b, i):
        at = lax.rem(b, TURN)
        return d_copy(part_out.at[b, lax.rem(d + i, n_d)], part_in.at[b], part_s.at[at], part_r.at[at], i)

    def part_all(b):
        at = lax.rem(b, TURN)
        return d_all(part_in.at[b], part_s.at[at], part_r.at[at])

    def hid_copy(b, i):
        at = lax.rem(b, TURN)
        return d_copy(hid.at[b], hid_in.at[b], hid_s.at[at], hid_r.at[at], i)

    def hid_all(b):
        at = lax.rem(b, TURN)
        return d_all(hid_in.at[b], hid_s.at[at], hid_r.at[at])

    def rs_copy(b, h, c):
        return remote(
            rs_out.at[b, h, c],
            rs_in.at[b + 1, h, c],
            rs_s.at[lax.rem(b, RING), h],
            rs_r.at[lax.rem(b + 1, RING), h, c],
            section=ring(h),
        )

    def rs_wait(b, h, c):
        at = lax.rem(b, RING)
        remote(rs_in.at[b, h, c], rs_in.at[b, h, c], rs_s.at[at, h], rs_r.at[at, h, c], section=ring(h)).wait_recv()

    def rs_sent(b, h):
        some = rs_out.at[b, h]
        remote(some, some, rs_s.at[lax.rem(b, RING), h], rs_r.at[0, h, 0], section=ring(h)).wait_send()

    unit = wg.shape[1] // n_d

    def gate_up(b):
        @pl.when(b >= TURN)
        def _():
            part_all(b - TURN).wait_send()

        block = jnp.concatenate([ag[b, :, c].reshape(rows, wide) for c in range(n_c)], axis=1)
        gate = dot(block, wg[...]).astype(BF16)
        upper = dot(block, wu[...]).astype(BF16)
        for p in range(n_d):
            part_out[b, p, :, 0:unit] = gate[:, p * unit : (p + 1) * unit]
            part_out[b, p, :, unit : 2 * unit] = upper[:, p * unit : (p + 1) * unit]
        for i in range(1, n_d):
            part_copy(b, i).start()

    def hidden_units(b):
        @pl.when(b == 0)
        def _():
            remote(sc.at[0, 1 - xh], sc.at[0, 1 - xh], sx_s, sx_r, section=across).wait_recv()

        @pl.when(b > 0)
        def _():
            for h in range(N_X):
                remote(
                    sc.at[b, h], sc.at[b, h], sc_s.at[0, h], sc_r.at[lax.rem(b, 2), h], section=ring(h)
                ).wait_recv()

        @pl.when((b > 1) & (b < n_y - 1))
        def _():
            for h in range(N_X):
                sc_copy(b - 2, h).wait_send()

        @pl.when(b < n_y - 1)
        def _():
            for h in range(N_X):
                sc_copy(b, h).start()

        @pl.when(b >= TURN)
        def _():
            hid_all(b - TURN).wait_send()

        scales = [jnp.sum(jnp.where(eye, sc[b, h][0:1, :], 0.0), axis=1, keepdims=True) for h in range(N_X)]
        both = part_out[b, d].astype(F32)
        part_all(b).wait_recv()
        for i in range(n_d - 1):
            both = both + part_in[b, i].astype(F32)
        both = both * jnp.concatenate(scales, axis=0)
        g = both[:, 0:unit]
        hid[b] = (g / (1.0 + jnp.exp(-g)) * both[:, unit : 2 * unit]).astype(BF16)
        for i in range(1, n_d):
            hid_copy(b, i).start()

    def down_product(b):
        hid_all(b).wait_recv()
        parts = [hid[b]] + [hid_in[b, i] for i in range(n_d - 1)]
        columns = []
        for p in range(n_d):
            value = parts[0]
            for i in range(1, n_d):
                value = jnp.where(lax.rem(d + n_d - i, n_d) == p, parts[i], value)
            columns.append(value)
        result = dot(jnp.concatenate(columns, axis=1), wd[...])

        def keep(ref):
            for h in range(N_X):
                for c in range(n_c):
                    ref[h, c] = result[h * cap : (h + 1) * cap, c * wide : (c + 1) * wide]

        @pl.when(b == 0)
        def _():
            keep(own)

        @pl.when(b > 0)
        def _():
            keep(res)

    def add_on(b, c):
        for h in range(N_X):

            @pl.when(b == 1)
            def _():
                rs_out[b, h, c] = res[h, c].astype(BF16)

            @pl.when(b > 1)
            def _():
                rs_wait(b, h, c)
                rs_out[b, h, c] = (res[h, c] + rs_in[b, h, c].astype(F32)).astype(BF16)

            rs_copy(b, h, c).start()

    def step(t, carry):
        @pl.when(t <= n_y)
        def _():
            gate_up(t - 1)

        @pl.when((t < n_y - 1) & (t >= RING))
        def _():
            for h in range(N_X):
                ag_sent(t - RING, h)

        for j in range(n_c):
            c = near_first[j]

            @pl.when(t < n_y)
            def _():
                for h in range(N_X):
                    ag_wait(t, h, c)

                    @pl.when(t < n_y - 1)
                    def _():
                        ag_copy(t, h, c).start()

            if j == 0:

                @pl.when(t > 4)
                def _():
                    add_on(t - 4, far_first[n_c - 1])

            if j == 1:

                @pl.when((t > 2) & (t < n_y + 3))
                def _():
                    down_product(t - 3)

                @pl.when((t >= 4 + RING) & (t < n_y + 3))
                def _():
                    for h in range(N_X):
                        rs_sent(t - 3 - RING, h)

            if j >= 1:

                @pl.when((t > 3) & (t < n_y + 3))
                def _():
                    add_on(t - 3, far_first[j - 1])

            if j == 1:

                @pl.when((t > 1) & (t < n_y + 2))
                def _():
                    hidden_units(t - 2)

        return carry

    lax.fori_loop(1, n_y + 4, step, 0)

    other = 1 - xh

    def xr_copy(c):
        return remote(xr_out.at[c], xr_in.at[c], xr_s, xr_r.at[c], section=across)

    for c in far_first:
        rs_wait(n_y, other, c)
        xr_out[c] = (own[other, c] + rs_in[n_y, other, c].astype(F32)).astype(BF16)
        xr_copy(c).start()
    for c in far_first:
        rs_wait(n_y, xh, c)
        answer = own[xh, c] + rs_in[n_y, xh, c].astype(F32)
        xr_copy(c).wait_recv()
        answer = answer + xr_in[c].astype(F32)
        for k in range(per):
            zp = c * per + k
            top, below = pack(answer[:, k * n_feat : (k + 1) * n_feat])
            bk_out[zp, 0:cap, :] = top.astype(BF16)
            bk_out[zp, cap : cap + low, :] = jnp.concatenate([below, jnp.zeros((8, LANES), F32)], axis=0).astype(BF16)

            @pl.when(zp != z)
            def _():
                z_copy(bk_out, bk_in, bk_s, bk_r, zp).start()

    bk_in[z] = bk_out[z]

    def z_all(src, send, recv):
        some = src.at[pl.ds(0, n_e - 1)]
        return remote(some, some, send, recv, expert=lax.rem(z + 1, n_e))

    z_all(bk_in, bk_s, bk_r).wait_recv()
    back_top = bk_in[:, 0:cap, :].reshape(n_e * cap, LANES)
    back_low = bk_in[:, cap : cap + low, :].reshape(n_e * low, LANES)
    out_ref[0:LANES, :] = (
        tok_ref[0:LANES, :].astype(F32) + dot_first(back_top, mix_top[0]) + dot_first(back_top, mix_top[1])
    ).astype(BF16)
    low_a = dot_first(back_low, mix_low[0]) + dot_first(back_low, mix_low[1])
    low_b = dot_first(back_low, mix_low[2]) + dot_first(back_low, mix_low[3])
    out_ref[LANES:n_feat, :] = (
        tok_ref[LANES:n_feat, :].astype(F32) + low_a[0:edge] + low_b[edge : 2 * edge]
    ).astype(BF16)

    z_all(go, go_s, go_r.at[0]).wait_send()
    z_all(bk_out, bk_s, bk_r).wait_send()
    d_all(ss_in, ss_s, ss_r).wait_send()
    sx_copy.wait_send()
    remote(ag.at[0, xh], ag.at[0, xh], x_s, x_r.at[0], section=across).wait_send()
    remote(xr_out, xr_out, xr_s, xr_r.at[0], section=across).wait_send()
    for h in range(N_X):
        for b in range(max(0, n_y - 3), n_y - 1):
            sc_copy(b, h).wait_send()
        for b in range(max(0, n_y - 1 - RING), n_y - 1):
            ag_sent(b, h)
        for b in range(max(1, n_y - RING), n_y):
            rs_sent(b, h)
    for b in range(max(0, n_y - TURN), n_y):
        part_all(b).wait_send()
        hid_all(b).wait_send()


def local(tokens, norm_gain, routes, gates, w_gate, w_up, w_down):
    n_tok, n_feat = tokens.shape
    n_e = lax.axis_size("expert")
    n_d = lax.axis_size("dp")
    n_y = lax.axis_size("section") // N_X
    n_c = min(CHUNKS, n_e)
    cap = min(n_tok, max(2, 3 * n_tok // n_e))
    low = cap // 2 + 8
    width = n_feat * n_e
    wide = width // n_c
    units = w_gate.shape[2]
    unit = units // n_d
    rows = N_X * cap
    dma = pltpu.SemaphoreType.DMA
    far = pl.BlockSpec(memory_space=pl.ANY)
    scratch = [
        pltpu.VMEM((n_feat, n_tok), BF16),
        pltpu.VMEM((1, n_feat), F32),
        pltpu.VMEM((2, n_tok), jnp.int32),
        pltpu.VMEM((2, n_tok), F32),
        pltpu.VMEM((width, units), BF16),
        pltpu.VMEM((width, units), BF16),
        pltpu.VMEM((units, width), BF16),
        dma((7,)),
        pltpu.VMEM((2, n_e * cap, n_tok), BF16),
        pltpu.VMEM((4, n_e * low, n_tok), BF16),
        pltpu.VMEM((n_e, cap + low, LANES), BF16),
        pltpu.VMEM((n_e, cap + low, LANES), BF16),
        pltpu.VMEM((8, LANES), F32),
        pltpu.VMEM((n_d - 1, 8, LANES), F32),
        pltpu.VMEM((n_y, N_X, 8, LANES), F32),
        pltpu.VMEM((n_y, N_X, n_c, cap, wide), BF16),
        pltpu.VMEM((n_y, n_d, rows, 2 * unit), BF16),
        pltpu.VMEM((n_y, n_d - 1, rows, 2 * unit), BF16),
        pltpu.VMEM((n_y, rows, unit), BF16),
        pltpu.VMEM((n_y, n_d - 1, rows, unit), BF16),
        pltpu.VMEM((N_X, n_c, cap, wide), F32),
        pltpu.VMEM((N_X, n_c, cap, wide), F32),
        pltpu.VMEM((n_y, N_X, n_c, cap, wide), BF16),
        pltpu.VMEM((n_y + 1, N_X, n_c, cap, wide), BF16),
        pltpu.VMEM((n_c, cap, wide), BF16),
        pltpu.VMEM((n_c, cap, wide), BF16),
        pltpu.VMEM((n_e, cap + low, LANES), BF16),
        pltpu.VMEM((n_e, cap + low, LANES), BF16),
        dma,
        dma((n_e,)),
        dma,
        dma,
        dma,
        dma,
        dma((2, N_X)),
        dma((2, N_X)),
        dma,
        dma((n_c,)),
        dma((RING, N_X)),
        dma((RING, N_X, n_c)),
        dma((TURN,)),
        dma((TURN,)),
        dma((TURN,)),
        dma((TURN,)),
        dma((RING, N_X)),
        dma((RING, N_X, n_c)),
        dma,
        dma((n_c,)),
        dma,
        dma,
    ]
    mixed = pl.pallas_call(
        functools.partial(kernel, (n_y, n_e, n_d, cap, n_c)),
        out_shape=jax.ShapeDtypeStruct((n_feat, n_tok), BF16),
        in_specs=[far] * 7,
        out_specs=pl.BlockSpec(memory_space=pltpu.VMEM),
        scratch_shapes=scratch,
        compiler_params=pltpu.CompilerParams(
            collective_id=0, has_side_effects=True, vmem_limit_bytes=64 * 1024 * 1024
        ),
        name="moe_layer",
    )(tokens.T, norm_gain.reshape(1, n_feat), routes.T, gates.T, w_gate, w_up, w_down)
    return mixed.T


def solution(mesh):
    in_specs = (
        P("section", ("dp", "expert")),
        P(("dp", "expert")),
        P("section", None),
        P("section", None),
        P("expert", "dp", "section"),
        P("expert", "dp", "section"),
        P("expert", "section", "dp"),
    )
    out_specs = P("section", ("dp", "expert"))
    return jax.shard_map(local, mesh=mesh, in_specs=in_specs, out_specs=out_specs, check_vma=False)
```

time: 88.4 us -> 83.5 us (0.945)
  Pallas kernels: 86.1 us -> 81.8 us
    pallas_call x1, Pallas kernels: 86.1 us -> 81.8 us  [local(): pl.pallas_call(functools.partial(kernel, (n_y, n_e, n_d, cap, n_c)), out_...]
where the time goes in v3:
time: 83.5 us; the launch traced here: 83.3 us
  Pallas kernels  81.8 us (98%)
  local copies, waits for them, and re-layouts  1.42 us (2%)
    pallas_call x1, Pallas kernels, local(): pl.pallas_call(functools.partial(kernel, (n_y, n_e, n_d, cap, n_c)), out_...  81.8 us

profile of v3, /device:TPU:1, one launch (start us, length us, event | category | flops | bytes accessed | tf_op | source)
XLA Modules:
  0.0 83.3 jit_solution(2190050099184794611)
XLA Ops:
  0.0 81.8 %moe_layer.1 = bf16[192,128]{1,0:T(8,128)(2,1)} custom-call(bf16[192,128]{1,0:T(8,128)(2,1)} %bitcast.6, f32[1,192]{1,0:T(1,128)} %bitcast.7, s32[2,128]{1,0:T(2,128)} %bitcast.8, f32[2,128]{1,0:T(2,128)} %bitcast.9, bf16[1,1536,512]{2,1,0:T(8,128)(2,1)} %wg_hbm.1, bf16[1,1536,512]{2,1,0:T(8,128)(2,1)} %wu_hbm.1, bf16[1,512,1536]{2,1,0:T(8,128)(2,1)} %wd_hbm.1), custom_call_target="tpu_custom_call" | custom-call | tf_op jit(solution)/shard_map/moe_layer/pallas_call | solution.py:589
  81.8 1.4 %copy.9 = bf16[128,192]{0,1:T(8,128)(2,1)} copy(bf16[128,192]{0,1:T(8,128)(2,1)} %bitcast.5) | data formatting | bytes 98304

commit v4 on v3

--- a/solution.py
+++ b/solution.py
@@ -16,6 +16,7 @@
 CHUNKS = 4
 RING = 3
 TURN = 4
+PAIR_AT, HIDDEN_AT, DOWN_AT = 1, 2, 3
 
 
 def dot(a, b):
@@ -70,11 +71,14 @@
     sc,
     ag,
     part_out,
-    part_in,
+    core_in,
+    pair_out,
+    pair_in,
     hid,
-    hid_in,
     own,
     res,
+    cross_out,
+    cross_in,
     rs_out,
     rs_in,
     xr_out,
@@ -93,12 +97,18 @@
     x_r,
     ag_s,
     ag_r,
-    part_s,
-    part_r,
+    ax_s,
+    ax_r,
+    core_s,
+    core_r,
+    pair_s,
+    pair_r,
     hid_s,
     hid_r,
     rs_s,
     rs_r,
+    rx_s,
+    rx_r,
     xr_s,
     xr_r,
     bk_s,
@@ -121,6 +131,9 @@
     up = xh * n_y + lax.rem(y + 1, n_y)
     down = xh * n_y + lax.rem(y + n_y - 1, n_y)
     across = (1 - xh) * n_y + y
+    other = 1 - xh
+    chip = lax.div(d, 2)
+    core = lax.rem(d, 2)
     mine = lax.div(z, per)
     spread = sorted(range(n_c), key=lambda i: min(i, n_c - i))
     near_first = [lax.rem(mine + i, n_c) for i in spread]
@@ -216,6 +229,9 @@
         at = lax.rem(b, RING)
         remote(ag.at[b, h, c], ag.at[b, h, c], ag_s.at[at, h], ag_r.at[at, h, c], section=ring(h)).wait_recv()
 
+    def ag_cross(c):
+        return remote(ag.at[n_y - 1, xh, c], ag.at[n_y - 1, xh, c], ax_s, ax_r, section=across)
+
     low_row = lax.broadcasted_iota(jnp.int32, (low, n_tok), 0)
     low_number = jnp.where(low_row < half, low_row, 4 * cap).astype(F32)
     for e in range(n_e):
@@ -264,8 +280,10 @@
     for i in range(1, n_d):
         d_copy(ss_out, ss_in, ss_s, ss_r, i).start()
     for c in near_first:
-        remote(ag.at[0, 1 - xh, c], ag.at[0, 1 - xh, c], x_s, x_r.at[c], section=across).wait_recv()
-        ag_copy(0, 1 - xh, c).start()
+        ag_wait(1, xh, c)
+        ag_copy(1, xh, c).start()
+        remote(ag.at[0, other, c], ag.at[0, other, c], x_s, x_r.at[c], section=across).wait_recv()
+        ag_copy(0, other, c).start()
     d_all(ss_in, ss_s, ss_r).wait_recv()
     total = row_squares
     for i in range(n_d - 1):
@@ -280,21 +298,17 @@
         at = lax.rem(b, 2)
         return remote(sc.at[b, h], sc.at[b + 1, h], sc_s.at[at, h], sc_r.at[1 - at, h], section=ring(h))
 
-    def part_copy(b, i):
+    def core_copy(b):
+        at = lax.rem(b, 2)
+        return remote(part_out.at[b, 1 - core], core_in.at[b], core_s.at[at], core_r.at[at], dp=2 * chip + 1 - core)
+
+    def pair_copy(b):
         at = lax.rem(b, TURN)
-        return d_copy(part_out.at[b, lax.rem(d + i, n_d)], part_in.at[b], part_s.at[at], part_r.at[at], i)
-
-    def part_all(b):
+        return remote(pair_out.at[b], pair_in.at[b], pair_s.at[at], pair_r.at[at], dp=2 * (1 - chip) + core)
+
+    def hid_copy(b, which):
         at = lax.rem(b, TURN)
-        return d_all(part_in.at[b], part_s.at[at], part_r.at[at])
-
-    def hid_copy(b, i):
-        at = lax.rem(b, TURN)
-        return d_copy(hid.at[b], hid_in.at[b], hid_s.at[at], hid_r.at[at], i)
-
-    def hid_all(b):
-        at = lax.rem(b, TURN)
-        return d_all(hid_in.at[b], hid_s.at[at], hid_r.at[at])
+        return remote(hid.at[b, which], hid.at[b, which], hid_s.at[at], hid_r.at[at], dp=2 * chip + 1 - core)
 
     def rs_copy(b, h, c):
         return remote(
@@ -313,21 +327,34 @@
         some = rs_out.at[b, h]
         remote(some, some, rs_s.at[lax.rem(b, RING), h], rs_r.at[0, h, 0], section=ring(h)).wait_send()
 
-    unit = wg.shape[1] // n_d
+    unit = wg.shape[1] // 2
 
     def gate_up(b):
-        @pl.when(b >= TURN)
-        def _():
-            part_all(b - TURN).wait_send()
+        @pl.when(b > 1)
+        def _():
+            core_copy(b - 2).wait_send()
+
+        @pl.when(b == n_y - 1)
+        def _():
+            last = ag.at[n_y - 1, other]
+            remote(last, last, ax_s, ax_r, section=across).wait_recv()
 
         block = jnp.concatenate([ag[b, :, c].reshape(rows, wide) for c in range(n_c)], axis=1)
         gate = dot(block, wg[...]).astype(BF16)
         upper = dot(block, wu[...]).astype(BF16)
-        for p in range(n_d):
+        for p in range(2):
             part_out[b, p, :, 0:unit] = gate[:, p * unit : (p + 1) * unit]
             part_out[b, p, :, unit : 2 * unit] = upper[:, p * unit : (p + 1) * unit]
-        for i in range(1, n_d):
-            part_copy(b, i).start()
+        core_copy(b).start()
+
+    def chip_sum(b):
+        @pl.when(b >= TURN)
+        def _():
+            pair_copy(b - TURN).wait_send()
+
+        core_copy(b).wait_recv()
+        pair_out[b] = (part_out[b, core].astype(F32) + core_in[b].astype(F32)).astype(BF16)
+        pair_copy(b).start()
 
     def hidden_units(b):
         @pl.when(b == 0)
@@ -353,29 +380,19 @@
 
         @pl.when(b >= TURN)
         def _():
-            hid_all(b - TURN).wait_send()
+            hid_copy(b - TURN, core).wait_send()
 
         scales = [jnp.sum(jnp.where(eye, sc[b, h][0:1, :], 0.0), axis=1, keepdims=True) for h in range(N_X)]
-        both = part_out[b, d].astype(F32)
-        part_all(b).wait_recv()
-        for i in range(n_d - 1):
-            both = both + part_in[b, i].astype(F32)
+        pair_copy(b).wait_recv()
+        both = part_out[b, core].astype(F32) + core_in[b].astype(F32) + pair_in[b].astype(F32)
         both = both * jnp.concatenate(scales, axis=0)
         g = both[:, 0:unit]
-        hid[b] = (g / (1.0 + jnp.exp(-g)) * both[:, unit : 2 * unit]).astype(BF16)
-        for i in range(1, n_d):
-            hid_copy(b, i).start()
+        hid[b, core] = (g / (1.0 + jnp.exp(-g)) * both[:, unit : 2 * unit]).astype(BF16)
+        hid_copy(b, core).start()
 
     def down_product(b):
-        hid_all(b).wait_recv()
-        parts = [hid[b]] + [hid_in[b, i] for i in range(n_d - 1)]
-        columns = []
-        for p in range(n_d):
-            value = parts[0]
-            for i in range(1, n_d):
-                value = jnp.where(lax.rem(d + n_d - i, n_d) == p, parts[i], value)
-            columns.append(value)
-        result = dot(jnp.concatenate(columns, axis=1), wd[...])
+        hid_copy(b, 1 - core).wait_recv()
+        result = dot(jnp.concatenate([hid[b, 0], hid[b, 1]], axis=1), wd[...])
 
         def keep(ref):
             for h in range(N_X):
@@ -388,91 +405,138 @@
 
         @pl.when(b > 0)
         def _():
-            keep(res)
-
-    def add_on(b, c):
-        for h in range(N_X):
-
-            @pl.when(b == 1)
+            keep(res.at[lax.rem(b, 2)])
+
+        @pl.when(b == 1)
+        def _():
+            for c in far_first:
+                cross_out[c] = res[1, other, c].astype(BF16)
+                rs_cross(c).start()
+
+    def rs_cross(c):
+        return remote(cross_out.at[c], cross_in.at[c], rx_s, rx_r.at[c], section=across)
+
+    def xr_copy(c):
+        return remote(xr_out.at[c], xr_in.at[c], xr_s, xr_r.at[c], section=across)
+
+    def add_own(b, c):
+        mine = res[lax.rem(b, 2), xh, c]
+
+        @pl.when(b == 1)
+        def _():
+            rs_cross(c).wait_recv()
+            rs_out[b, xh, c] = (mine + cross_in[c].astype(F32)).astype(BF16)
+
+        @pl.when(b > 1)
+        def _():
+            rs_wait(b, xh, c)
+            rs_out[b, xh, c] = (mine + rs_in[b, xh, c].astype(F32)).astype(BF16)
+
+        rs_copy(b, xh, c).start()
+
+    def add_other(b, c):
+        @pl.when(b < n_y)
+        def _():
+            mine = res[lax.rem(b, 2), other, c]
+
+            @pl.when(b == 2)
             def _():
-                rs_out[b, h, c] = res[h, c].astype(BF16)
-
-            @pl.when(b > 1)
+                rs_out[b, other, c] = mine.astype(BF16)
+
+            @pl.when(b > 2)
             def _():
-                rs_wait(b, h, c)
-                rs_out[b, h, c] = (res[h, c] + rs_in[b, h, c].astype(F32)).astype(BF16)
-
-            rs_copy(b, h, c).start()
+                rs_wait(b, other, c)
+                rs_out[b, other, c] = (mine + rs_in[b, other, c].astype(F32)).astype(BF16)
+
+            rs_copy(b, other, c).start()
+
+        @pl.when(b == n_y)
+        def _():
+            rs_wait(n_y, other, c)
+            xr_out[c] = (own[other, c] + rs_in[n_y, other, c].astype(F32)).astype(BF16)
+            xr_copy(c).start()
+
+    def add_on(t, c):
+        @pl.when((t > 3) & (t < n_y + 3))
+        def _():
+            add_own(t - 3, c)
+            add_other(t - 2, c)
 
     def step(t, carry):
         @pl.when(t <= n_y)
         def _():
             gate_up(t - 1)
 
-        @pl.when((t < n_y - 1) & (t >= RING))
-        def _():
-            for h in range(N_X):
-                ag_sent(t - RING, h)
+        @pl.when((t > 1) & (t < n_y - 2))
+        def _():
+            ag_sent(t - 2, xh)
+
+        @pl.when((t >= RING) & (t < n_y - 2))
+        def _():
+            ag_sent(t - RING, other)
 
         for j in range(n_c):
             c = near_first[j]
 
-            @pl.when(t < n_y)
+            @pl.when(t < n_y - 1)
             def _():
-                for h in range(N_X):
-                    ag_wait(t, h, c)
-
-                    @pl.when(t < n_y - 1)
-                    def _():
-                        ag_copy(t, h, c).start()
-
-            if j == 0:
-
-                @pl.when(t > 4)
-                def _():
-                    add_on(t - 4, far_first[n_c - 1])
-
-            if j == 1:
-
-                @pl.when((t > 2) & (t < n_y + 3))
-                def _():
-                    down_product(t - 3)
-
-                @pl.when((t >= 4 + RING) & (t < n_y + 3))
-                def _():
-                    for h in range(N_X):
-                        rs_sent(t - 3 - RING, h)
-
-            if j >= 1:
-
-                @pl.when((t > 3) & (t < n_y + 3))
-                def _():
-                    add_on(t - 3, far_first[j - 1])
-
-            if j == 1:
+                ag_wait(t + 1, xh, c)
+
+                @pl.when(t < n_y - 2)
+                def _():
+                    ag_copy(t + 1, xh, c).start()
+
+                @pl.when(t == n_y - 2)
+                def _():
+                    ag_cross(c).start()
+
+                ag_wait(t, other, c)
+
+                @pl.when(t < n_y - 2)
+                def _():
+                    ag_copy(t, other, c).start()
+
+            if j == min(PAIR_AT, n_c - 1):
+
+                @pl.when(t <= n_y)
+                def _():
+                    chip_sum(t - 1)
+
+            if j == min(HIDDEN_AT, n_c - 1):
 
                 @pl.when((t > 1) & (t < n_y + 2))
                 def _():
                     hidden_units(t - 2)
 
+            if j == down_at:
+
+                @pl.when((t > 1) & (t < n_y + 2))
+                def _():
+                    down_product(t - 2)
+
+                @pl.when((t > 3 + RING) & (t < n_y + 3))
+                def _():
+                    rs_sent(t - 3 - RING, xh)
+
+                @pl.when((t > 3 + RING) & (t < n_y + 2))
+                def _():
+                    rs_sent(t - 2 - RING, other)
+
+            if j >= down_at:
+                add_on(t, far_first[j - down_at])
+            else:
+                add_on(t - 1, far_first[j - down_at + n_c])
+
         return carry
 
+    down_at = min(DOWN_AT, n_c - 1)
     lax.fori_loop(1, n_y + 4, step, 0)
 
-    other = 1 - xh
-
-    def xr_copy(c):
-        return remote(xr_out.at[c], xr_in.at[c], xr_s, xr_r.at[c], section=across)
-
     for c in far_first:
-        rs_wait(n_y, other, c)
-        xr_out[c] = (own[other, c] + rs_in[n_y, other, c].astype(F32)).astype(BF16)
-        xr_copy(c).start()
-    for c in far_first:
+        xr_copy(c).wait_recv()
+        answer = own[xh, c] + xr_in[c].astype(F32)
         rs_wait(n_y, xh, c)
-        answer = own[xh, c] + rs_in[n_y, xh, c].astype(F32)
-        xr_copy(c).wait_recv()
-        answer = answer + xr_in[c].astype(F32)
+        answer = answer + rs_in[n_y, xh, c].astype(F32)
         for k in range(per):
             zp = c * per + k
             top, below = pack(answer[:, k * n_feat : (k + 1) * n_feat])
@@ -510,13 +574,21 @@
     for h in range(N_X):
         for b in range(max(0, n_y - 3), n_y - 1):
             sc_copy(b, h).wait_send()
-        for b in range(max(0, n_y - 1 - RING), n_y - 1):
-            ag_sent(b, h)
-        for b in range(max(1, n_y - RING), n_y):
-            rs_sent(b, h)
+    for b in range(max(0, n_y - 1 - RING), n_y - 1):
+        ag_sent(b, xh)
+    for b in range(max(0, n_y - 2 - RING), n_y - 2):
+        ag_sent(b, other)
+    for b in range(max(1, n_y - RING), n_y):
+        rs_sent(b, xh)
+    for b in range(max(2, n_y - RING), n_y):
+        rs_sent(b, other)
+    remote(ag.at[n_y - 1, xh], ag.at[n_y - 1, xh], ax_s, ax_r, section=across).wait_send()
+    remote(cross_out, cross_out, rx_s, rx_r.at[0], section=across).wait_send()
+    for b in range(n_y - 2, n_y):
+        core_copy(b).wait_send()
     for b in range(max(0, n_y - TURN), n_y):
-        part_all(b).wait_send()
-        hid_all(b).wait_send()
+        pair_copy(b).wait_send()
+        hid_copy(b, core).wait_send()
 
 
 def local(tokens, norm_gain, routes, gates, w_gate, w_up, w_down):
@@ -530,7 +602,7 @@
     width = n_feat * n_e
     wide = width // n_c
     units = w_gate.shape[2]
-    unit = units // n_d
+    unit = units // 2
     rows = N_X * cap
     dma = pltpu.SemaphoreType.DMA
     far = pl.BlockSpec(memory_space=pl.ANY)
@@ -551,12 +623,15 @@
         pltpu.VMEM((n_d - 1, 8, LANES), F32),
         pltpu.VMEM((n_y, N_X, 8, LANES), F32),
         pltpu.VMEM((n_y, N_X, n_c, cap, wide), BF16),
-        pltpu.VMEM((n_y, n_d, rows, 2 * unit), BF16),
-        pltpu.VMEM((n_y, n_d - 1, rows, 2 * unit), BF16),
-        pltpu.VMEM((n_y, rows, unit), BF16),
-        pltpu.VMEM((n_y, n_d - 1, rows, unit), BF16),
+        pltpu.VMEM((n_y, 2, rows, 2 * unit), BF16),
+        pltpu.VMEM((n_y, rows, 2 * unit), BF16),
+        pltpu.VMEM((n_y, rows, 2 * unit), BF16),
+        pltpu.VMEM((n_y, rows, 2 * unit), BF16),
+        pltpu.VMEM((n_y, 2, rows, unit), BF16),
         pltpu.VMEM((N_X, n_c, cap, wide), F32),
-        pltpu.VMEM((N_X, n_c, cap, wide), F32),
+        pltpu.VMEM((2, N_X, n_c, cap, wide), F32),
+        pltpu.VMEM((n_c, cap, wide), BF16),
+        pltpu.VMEM((n_c, cap, wide), BF16),
         pltpu.VMEM((n_y, N_X, n_c, cap, wide), BF16),
         pltpu.VMEM((n_y + 1, N_X, n_c, cap, wide), BF16),
         pltpu.VMEM((n_c, cap, wide), BF16),
@@ -575,12 +650,18 @@
         dma((n_c,)),
         dma((RING, N_X)),
         dma((RING, N_X, n_c)),
+        dma,
+        dma,
+        dma((2,)),
+        dma((2,)),
         dma((TURN,)),
         dma((TURN,)),
         dma((TURN,)),
         dma((TURN,)),
         dma((RING, N_X)),
         dma((RING, N_X, n_c)),
+        dma,
+        dma((n_c,)),
         dma,
         dma((n_c,)),
         dma,

time: 83.5 us -> 78.3 us (0.938)
  Pallas kernels: 81.8 us -> 76.7 us
    pallas_call x1, Pallas kernels: 81.8 us -> 76.7 us  [local(): pl.pallas_call(functools.partial(kernel, (n_y, n_e, n_d, cap, n_c)), out_...]
where the time goes in v4:
time: 78.3 us; the launch traced here: 78.2 us
  Pallas kernels  76.7 us (98%)
  local copies, waits for them, and re-layouts  1.42 us (2%)
    pallas_call x1, Pallas kernels, local(): pl.pallas_call(functools.partial(kernel, (n_y, n_e, n_d, cap, n_c)), out_...  76.7 us

profile of v4, /device:TPU:1, one launch (start us, length us, event | category | flops | bytes accessed | tf_op | source)
XLA Modules:
  0.0 78.2 jit_solution(16441969946685494796)
XLA Ops:
  0.0 76.7 %moe_layer.1 = bf16[192,128]{1,0:T(8,128)(2,1)} custom-call(bf16[192,128]{1,0:T(8,128)(2,1)} %bitcast.6, f32[1,192]{1,0:T(1,128)} %bitcast.7, s32[2,128]{1,0:T(2,128)} %bitcast.8, f32[2,128]{1,0:T(2,128)} %bitcast.9, bf16[1,1536,512]{2,1,0:T(8,128)(2,1)} %wg_hbm.1, bf16[1,1536,512]{2,1,0:T(8,128)(2,1)} %wu_hbm.1, bf16[1,512,1536]{2,1,0:T(8,128)(2,1)} %wd_hbm.1), custom_call_target="tpu_custom_call" | custom-call | tf_op jit(solution)/shard_map/moe_layer/pallas_call | solution.py:670
  76.7 1.4 %copy.9 = bf16[128,192]{0,1:T(8,128)(2,1)} copy(bf16[128,192]{0,1:T(8,128)(2,1)} %bitcast.5) | data formatting | bytes 98304

commit v5 on v4

--- a/solution.py
+++ b/solution.py
@@ -16,7 +16,7 @@
 CHUNKS = 4
 RING = 3
 TURN = 4
-PAIR_AT, HIDDEN_AT, DOWN_AT = 1, 2, 3
+PAIR_AT, HIDDEN_AT, DOWN_AT = 1, 3, 4
 
 
 def dot(a, b):
@@ -79,6 +79,8 @@
     res,
     cross_out,
     cross_in,
+    straight_out,
+    straight_in,
     rs_out,
     rs_in,
     xr_out,
@@ -97,6 +99,8 @@
     x_r,
     ag_s,
     ag_r,
+    dr_s,
+    dr_r,
     ax_s,
     ax_r,
     core_s,
@@ -109,6 +113,8 @@
     rs_r,
     rx_s,
     rx_r,
+    dt_s,
+    dt_r,
     xr_s,
     xr_r,
     bk_s,
@@ -209,7 +215,7 @@
     def z_copy(src, dst, send, recv, to):
         return remote(src.at[to], dst.at[z], send, recv, expert=to)
 
-    for i in order:
+    for i in order[::-1]:
         z_copy(go, got, go_s, go_r.at[z], lax.rem(z + i, n_e)).start()
     got[z] = go[z]
 
@@ -229,8 +235,11 @@
         at = lax.rem(b, RING)
         remote(ag.at[b, h, c], ag.at[b, h, c], ag_s.at[at, h], ag_r.at[at, h, c], section=ring(h)).wait_recv()
 
-    def ag_cross(c):
-        return remote(ag.at[n_y - 1, xh, c], ag.at[n_y - 1, xh, c], ax_s, ax_r, section=across)
+    def ag_straight(c):
+        return remote(ag.at[0, xh, c], ag.at[n_y - 1, xh, c], dr_s, dr_r, section=ring(other))
+
+    def ag_last(send, recv, **where):
+        return remote(ag.at[n_y - 1, xh], ag.at[n_y - 1, xh], send, recv, **where)
 
     low_row = lax.broadcasted_iota(jnp.int32, (low, n_tok), 0)
     low_number = jnp.where(low_row < half, low_row, 4 * cap).astype(F32)
@@ -269,6 +278,7 @@
         ag[0, xh, c] = jnp.concatenate(pieces, axis=1).astype(BF16)
         x_copy(c).start()
         ag_copy(0, xh, c).start()
+        ag_straight(c).start()
 
     def d_copy(src, dst, send, recv, i):
         return remote(src, dst.at[i - 1], send, recv, dp=lax.rem(d + i, n_d))
@@ -419,15 +429,17 @@
     def xr_copy(c):
         return remote(xr_out.at[c], xr_in.at[c], xr_s, xr_r.at[c], section=across)
 
+    def straight_copy(c):
+        return remote(straight_out.at[c], straight_in.at[c], dt_s, dt_r.at[c], section=ring(other))
+
     def add_own(b, c):
         mine = res[lax.rem(b, 2), xh, c]
 
-        @pl.when(b == 1)
-        def _():
-            rs_cross(c).wait_recv()
-            rs_out[b, xh, c] = (mine + cross_in[c].astype(F32)).astype(BF16)
-
-        @pl.when(b > 1)
+        @pl.when(b == 2)
+        def _():
+            rs_out[b, xh, c] = mine.astype(BF16)
+
+        @pl.when(b > 2)
         def _():
             rs_wait(b, xh, c)
             rs_out[b, xh, c] = (mine + rs_in[b, xh, c].astype(F32)).astype(BF16)
@@ -459,15 +471,40 @@
     def add_on(t, c):
         @pl.when((t > 3) & (t < n_y + 3))
         def _():
+            add_other(t - 2, c)
+
+        @pl.when((t > 4) & (t < n_y + 3))
+        def _():
             add_own(t - 3, c)
-            add_other(t - 2, c)
+
+        @pl.when(t == 4)
+        def _():
+            rs_cross(c).wait_recv()
+            straight_out[c] = (res[1, xh, c] + cross_in[c].astype(F32)).astype(BF16)
+
+        @pl.when(t == n_y + 2)
+        def _():
+            straight_copy(c).start()
+
+    def down_step(t):
+        @pl.when((t > 1) & (t < n_y + 2))
+        def _():
+            down_product(t - 2)
+
+        @pl.when((t > 4 + RING) & (t < n_y + 3))
+        def _():
+            rs_sent(t - 3 - RING, xh)
+
+        @pl.when((t > 3 + RING) & (t < n_y + 2))
+        def _():
+            rs_sent(t - 2 - RING, other)
 
     def step(t, carry):
         @pl.when(t <= n_y)
         def _():
             gate_up(t - 1)
 
-        @pl.when((t > 1) & (t < n_y - 2))
+        @pl.when((t > 1) & (t < n_y - 3))
         def _():
             ag_sent(t - 2, xh)
 
@@ -480,22 +517,27 @@
 
             @pl.when(t < n_y - 1)
             def _():
-                ag_wait(t + 1, xh, c)
-
-                @pl.when(t < n_y - 2)
-                def _():
-                    ag_copy(t + 1, xh, c).start()
-
-                @pl.when(t == n_y - 2)
-                def _():
-                    ag_cross(c).start()
-
                 ag_wait(t, other, c)
 
                 @pl.when(t < n_y - 2)
                 def _():
                     ag_copy(t, other, c).start()
 
+            @pl.when(t < n_y - 2)
+            def _():
+                ag_wait(t + 1, xh, c)
+
+                @pl.when(t < n_y - 3)
+                def _():
+                    ag_copy(t + 1, xh, c).start()
+
+            if j == n_c - 1:
+
+                @pl.when(t == 1)
+                def _():
+                    ag_last(dr_s, dr_r, section=ring(other)).wait_recv()
+                    ag_last(ax_s, ax_r, section=across).start()
+
             if j == min(PAIR_AT, n_c - 1):
 
                 @pl.when(t <= n_y)
@@ -509,34 +551,25 @@
                     hidden_units(t - 2)
 
             if j == down_at:
-
-                @pl.when((t > 1) & (t < n_y + 2))
-                def _():
-                    down_product(t - 2)
-
-                @pl.when((t > 3 + RING) & (t < n_y + 3))
-                def _():
-                    rs_sent(t - 3 - RING, xh)
-
-                @pl.when((t > 3 + RING) & (t < n_y + 2))
-                def _():
-                    rs_sent(t - 2 - RING, other)
+                down_step(t - down_late)
 
             if j >= down_at:
-                add_on(t, far_first[j - down_at])
+                add_on(t - down_late, far_first[j - down_at])
             else:
-                add_on(t - 1, far_first[j - down_at + n_c])
+                add_on(t - down_late - 1, far_first[j - down_at + n_c])
 
         return carry
 
-    down_at = min(DOWN_AT, n_c - 1)
-    lax.fori_loop(1, n_y + 4, step, 0)
+    down_late, down_at = divmod(DOWN_AT * n_c // CHUNKS, n_c)
+    lax.fori_loop(1, n_y + 3 + down_late + (down_at > 0), step, 0)
 
     for c in far_first:
         xr_copy(c).wait_recv()
         answer = own[xh, c] + xr_in[c].astype(F32)
         rs_wait(n_y, xh, c)
         answer = answer + rs_in[n_y, xh, c].astype(F32)
+        straight_copy(c).wait_recv()
+        answer = answer + straight_in[c].astype(F32)
         for k in range(per):
             zp = c * per + k
             top, below = pack(answer[:, k * n_feat : (k + 1) * n_feat])
@@ -574,15 +607,15 @@
     for h in range(N_X):
         for b in range(max(0, n_y - 3), n_y - 1):
             sc_copy(b, h).wait_send()
-    for b in range(max(0, n_y - 1 - RING), n_y - 1):
+    for b in range(max(0, n_y - 2 - RING), n_y - 2):
         ag_sent(b, xh)
-    for b in range(max(0, n_y - 2 - RING), n_y - 2):
         ag_sent(b, other)
-    for b in range(max(1, n_y - RING), n_y):
+    for b in range(max(2, n_y - RING), n_y):
         rs_sent(b, xh)
-    for b in range(max(2, n_y - RING), n_y):
         rs_sent(b, other)
-    remote(ag.at[n_y - 1, xh], ag.at[n_y - 1, xh], ax_s, ax_r, section=across).wait_send()
+    ag_last(dr_s, dr_r, section=ring(other)).wait_send()
+    ag_last(ax_s, ax_r, section=across).wait_send()
+    remote(straight_out, straight_out, dt_s, dt_r.at[0], section=ring(other)).wait_send()
     remote(cross_out, cross_out, rx_s, rx_r.at[0], section=across).wait_send()
     for b in range(n_y - 2, n_y):
         core_copy(b).wait_send()
@@ -632,6 +665,8 @@
         pltpu.VMEM((2, N_X, n_c, cap, wide), F32),
         pltpu.VMEM((n_c, cap, wide), BF16),
         pltpu.VMEM((n_c, cap, wide), BF16),
+        pltpu.VMEM((n_c, cap, wide), BF16),
+        pltpu.VMEM((n_c, cap, wide), BF16),
         pltpu.VMEM((n_y, N_X, n_c, cap, wide), BF16),
         pltpu.VMEM((n_y + 1, N_X, n_c, cap, wide), BF16),
         pltpu.VMEM((n_c, cap, wide), BF16),
@@ -650,6 +685,8 @@
         dma((n_c,)),
         dma((RING, N_X)),
         dma((RING, N_X, n_c)),
+        dma,
+        dma,
         dma,
         dma,
         dma((2,)),
@@ -660,6 +697,8 @@
         dma((TURN,)),
         dma((RING, N_X)),
         dma((RING, N_X, n_c)),
+        dma,
+        dma((n_c,)),
         dma,
         dma((n_c,)),
         dma,

time: 78.3 us -> 77.5 us (0.990)
  Pallas kernels: 76.7 us -> 75.5 us
    pallas_call x1, Pallas kernels: 76.7 us -> 75.5 us  [local(): pl.pallas_call(functools.partial(kernel, (n_y, n_e, n_d, cap, n_c)), out_...]
where the time goes in v5:
time: 77.5 us; the launch traced here: 76.9 us
  Pallas kernels  75.5 us (97%)
  local copies, waits for them, and re-layouts  1.42 us (2%)
    pallas_call x1, Pallas kernels, local(): pl.pallas_call(functools.partial(kernel, (n_y, n_e, n_d, cap, n_c)), out_...  75.5 us

profile of v5, /device:TPU:1, one launch (start us, length us, event | category | flops | bytes accessed | tf_op | source)
XLA Modules:
  0.0 76.9 jit_solution(14660814777881954222)
XLA Ops:
  0.0 75.5 %moe_layer.1 = bf16[192,128]{1,0:T(8,128)(2,1)} custom-call(bf16[192,128]{1,0:T(8,128)(2,1)} %bitcast.6, f32[1,192]{1,0:T(1,128)} %bitcast.7, s32[2,128]{1,0:T(2,128)} %bitcast.8, f32[2,128]{1,0:T(2,128)} %bitcast.9, bf16[1,1536,512]{2,1,0:T(8,128)(2,1)} %wg_hbm.1, bf16[1,1536,512]{2,1,0:T(8,128)(2,1)} %wu_hbm.1, bf16[1,512,1536]{2,1,0:T(8,128)(2,1)} %wd_hbm.1), custom_call_target="tpu_custom_call" | custom-call | tf_op jit(solution)/shard_map/moe_layer/pallas_call | solution.py:709
  75.5 1.4 %copy.9 = bf16[128,192]{0,1:T(8,128)(2,1)} copy(bf16[128,192]{0,1:T(8,128)(2,1)} %bitcast.5) | data formatting | bytes 98304

commit v6 on v5

--- a/solution.py
+++ b/solution.py
@@ -277,8 +277,8 @@
             row_squares = row_squares + (terms[0:1] + terms[1:2] + terms[2:3])
         ag[0, xh, c] = jnp.concatenate(pieces, axis=1).astype(BF16)
         x_copy(c).start()
+        ag_straight(c).start()
         ag_copy(0, xh, c).start()
-        ag_straight(c).start()
 
     def d_copy(src, dst, send, recv, i):
         return remote(src, dst.at[i - 1], send, recv, dp=lax.rem(d + i, n_d))
@@ -500,10 +500,6 @@
             rs_sent(t - 2 - RING, other)
 
     def step(t, carry):
-        @pl.when(t <= n_y)
-        def _():
-            gate_up(t - 1)
-
         @pl.when((t > 1) & (t < n_y - 3))
         def _():
             ag_sent(t - 2, xh)
@@ -537,6 +533,12 @@
                 def _():
                     ag_last(dr_s, dr_r, section=ring(other)).wait_recv()
                     ag_last(ax_s, ax_r, section=across).start()
+
+            if j == 0:
+
+                @pl.when(t <= n_y)
+                def _():
+                    gate_up(t - 1)
 
             if j == min(PAIR_AT, n_c - 1):
 

time: 77.5 us -> 77.6 us (level)
  no operation moved by 1% of the time
where the time goes in v6:
time: 77.6 us; the launch traced here: 76.7 us
  Pallas kernels  75.3 us (97%)
  local copies, waits for them, and re-layouts  1.42 us (2%)
    pallas_call x1, Pallas kernels, local(): pl.pallas_call(functools.partial(kernel, (n_y, n_e, n_d, cap, n_c)), out_...  75.3 us

profile of v6, /device:TPU:1, one launch (start us, length us, event | category | flops | bytes accessed | tf_op | source)
XLA Modules:
  0.0 76.7 jit_solution(17444929001521409948)
XLA Ops:
  0.0 75.3 %moe_layer.1 = bf16[192,128]{1,0:T(8,128)(2,1)} custom-call(bf16[192,128]{1,0:T(8,128)(2,1)} %bitcast.6, f32[1,192]{1,0:T(1,128)} %bitcast.7, s32[2,128]{1,0:T(2,128)} %bitcast.8, f32[2,128]{1,0:T(2,128)} %bitcast.9, bf16[1,1536,512]{2,1,0:T(8,128)(2,1)} %wg_hbm.1, bf16[1,1536,512]{2,1,0:T(8,128)(2,1)} %wu_hbm.1, bf16[1,512,1536]{2,1,0:T(8,128)(2,1)} %wd_hbm.1), custom_call_target="tpu_custom_call" | custom-call | tf_op jit(solution)/shard_map/moe_layer/pallas_call | solution.py:711
  75.3 1.4 %copy.9 = bf16[128,192]{0,1:T(8,128)(2,1)} copy(bf16[128,192]{0,1:T(8,128)(2,1)} %bitcast.5) | data formatting | bytes 98304
